TPU v7x, 512 devices: a whole 4x4x16 slice. The times are simulated.
512 devices in a mesh: dp: 16 (over z), seq: 32 (over x, y, core).
Axes of the slice: x: 4, y: 4, z: 16, core: 2. Of those that a mesh axis runs over, the one named last changes fastest.
Arguments:
- latents: bfloat16 [16, 4096, 3072], P('dp', 'seq'), may hold values from -6 to 6
- modulation_shift: bfloat16 [16, 3, 3072], P('dp'), may hold values from -3 to 3
- modulation_scale: bfloat16 [16, 3, 3072], P('dp'), may hold values from -1.5 to 1.5
- query: bfloat16 [16, 4096, 3072], P('dp', 'seq'), may hold values from -6 to 6
- key: bfloat16 [16, 4096, 3072], P('dp', 'seq'), may hold values from -6 to 6
- value: bfloat16 [16, 4096, 3072], P('dp', 'seq'), may hold values from -6 to 6
- adapter_down_weight: bfloat16 [3072, 128], replicated, may hold values from -0.109375 to 0.109375
- adapter_up_weight: bfloat16 [128, 3072], replicated, may hold values from -1.5 to 1.5
- adapter_index: int32 [16, 4096, 2], P('dp', 'seq'), may hold values from 0 to 7, all different within a row
- adapter_weight: float32 [16, 4096, 2], P('dp', 'seq'), may hold values from 0.3 to 1.2
- sequence_length: int32 [16, 3], P('dp'), may hold values from 1 to 3072, 4096 in all within a row
Outputs:
- attended: bfloat16 [16, 4096, 3072], P('dp', 'seq')
Inputs may be any that keep to these rules, and one draw needn't show every extreme that they name: `sequence_length`: each pack's lengths sum to 4096 and its longest sequence has exactly 3072 tokens. `adapter_index`: the 2 LoRAs of a token are different.
All inputs are finite; a program needn't handle non-finite values.
Results may differ from a plain program's by a relative error of at most 0.0058.
Values may be sent and summed in bfloat16 or wider, within the bound.
No kernel may reach another device: no remote copies, remote signals or barrier semaphores. Data moves between devices by JAX's collectives and lax.ppermute only.
A program may use at most 128 MiB of HBM per device.

v0:
```python
import math

import jax
import jax.numpy as jnp
from jax import lax
from jax.sharding import PartitionSpec as P

HEADS = 24
HEAD_DIM = 128
STYLE_ADAPTERS = 8
HEAD_GROUPS = 8


mask_value = -1e30
epsilon = 1e-06


def segment_of(positions, lengths):
    bounds = jnp.cumsum(lengths)[:-1]
    return jnp.sum((positions[:, None] >= bounds[None, :]).astype(jnp.int32), axis=1)


def to_groups(rows_in, parts):
    total, width_all = rows_in.shape
    width = width_all // HEAD_GROUPS
    shaped = rows_in.reshape(parts, total // parts, HEAD_GROUPS, width)
    return shaped.transpose(0, 2, 1, 3).reshape(parts * HEAD_GROUPS, total // parts, width)


def to_copies(rows_in, parts):
    total, width_all = rows_in.shape
    width = width_all // HEAD_GROUPS
    shaped = rows_in.reshape(total, HEAD_GROUPS, width).transpose(1, 0, 2)
    spread = jnp.broadcast_to(shaped[None], (parts, HEAD_GROUPS, total, width))
    return spread.reshape(parts * HEAD_GROUPS, total, width)


def block_update(state, queries, query_seg, keys, value_rows, key_seg):
    query_count, heads, depth = queries.shape
    key_count = keys.shape[0]
    query_block = math.gcd(query_count, 512)
    key_block = math.gcd(key_count, 512)
    factor = 1.0 / math.sqrt(depth)
    query_blocks = queries.reshape(query_count // query_block, query_block, heads, depth)
    query_segs = query_seg.reshape(query_count // query_block, query_block)
    key_blocks = keys.reshape(key_count // key_block, key_block, heads, depth)
    value_blocks = value_rows.reshape(key_count // key_block, key_block, heads, depth)
    key_segs = key_seg.reshape(key_count // key_block, key_block)
    largest, totals, accum = state

    def per_query(items):
        query_tile, query_tile_seg, start_max, start_total, start_accum = items

        def visit(carry, key_items):
            key_tile, value_tile, key_tile_seg = key_items
            old_max, old_total, old_accum = carry
            scores = (
                jnp.einsum("qhd,khd->hqk", query_tile, key_tile, preferred_element_type=jnp.float32)
                * factor
            )
            same = query_tile_seg[:, None] == key_tile_seg[None, :]
            scores = jnp.where(same[None], scores, mask_value)
            new_max = jnp.maximum(old_max, jnp.max(scores, axis=2))
            rescale = jnp.exp(old_max - new_max)
            expo = jnp.exp(scores - new_max[:, :, None])
            new_total = old_total * rescale + jnp.sum(expo, axis=2)
            new_accum = old_accum * rescale[:, :, None] + jnp.einsum(
                "hqk,khd->hqd",
                expo.astype(jnp.bfloat16),
                value_tile,
                preferred_element_type=jnp.float32,
            )
            carry = (new_max, new_total, new_accum)
            return (carry, None)

        result, _ = lax.scan(
            visit, (start_max, start_total, start_accum), (key_blocks, value_blocks, key_segs)
        )
        return result

    return lax.map(per_query, (query_blocks, query_segs, largest, totals, accum))


def body(
    latents,
    modulation_shift,
    modulation_scale,
    query,
    key,
    value,
    adapter_down_weight,
    adapter_up_weight,
    adapter_index,
    adapter_weight,
    sequence_length,
):
    rows = latents.shape[1]
    width_all = latents.shape[2]
    n_seq = lax.axis_size("seq")
    parts = n_seq // HEAD_GROUPS
    sub_rows = rows // parts
    device = lax.axis_index("seq")
    part_row = device // HEAD_GROUPS
    lengths = sequence_length[0]
    own_pos = device * rows + jnp.arange(rows, dtype=jnp.int32)
    own_seg = segment_of(own_pos, lengths)
    floats = latents[0].astype(jnp.float32)
    center = jnp.mean(floats, axis=1, keepdims=True)
    variance = jnp.mean(jnp.square(floats - center), axis=1, keepdims=True)
    normed = (floats - center) / jnp.sqrt(variance + epsilon)
    onehot = (own_seg[:, None] == jnp.arange(lengths.shape[0], dtype=jnp.int32)[None, :]).astype(
        jnp.bfloat16
    )
    shift_rows = jnp.dot(onehot, modulation_shift[0], preferred_element_type=jnp.float32)
    scale_rows = jnp.dot(onehot, modulation_scale[0], preferred_element_type=jnp.float32)
    modulated_input = ((1.0 + scale_rows) * normed + shift_rows).astype(jnp.bfloat16)
    selected_adapter = (
        adapter_index[0][:, :, None] == jnp.arange(STYLE_ADAPTERS, dtype=jnp.int32)[None, None, :]
    ).astype(jnp.float32)
    mixing_weight = jnp.sum(adapter_weight[0][:, :, None] * selected_adapter, axis=1)
    rank_position = adapter_down_weight.shape[1] // STYLE_ADAPTERS
    spread_coef = jnp.repeat(mixing_weight, rank_position, axis=1)
    reduced_value = jnp.dot(
        modulated_input, adapter_down_weight, preferred_element_type=jnp.float32
    )
    weighted_update = (reduced_value * spread_coef).astype(jnp.bfloat16)
    value_update = jnp.dot(weighted_update, adapter_up_weight, preferred_element_type=jnp.float32)
    blended_values = (value[0].astype(jnp.float32) + value_update).astype(jnp.bfloat16)
    heads_here = HEADS // HEAD_GROUPS
    query_count = n_seq * sub_rows
    grouped = lax.all_to_all(
        to_groups(query[0], parts), "seq", split_axis=0, concat_axis=0, tiled=True
    )
    queries_here = grouped.reshape(query_count, heads_here, HEAD_DIM)
    sources = jnp.arange(n_seq, dtype=jnp.int32)[:, None] * rows
    query_seg = segment_of(
        (sources + part_row * sub_rows + jnp.arange(sub_rows, dtype=jnp.int32)[None, :]).reshape(
            -1
        ),
        lengths,
    )
    query_block = math.gcd(query_count, 512)
    block_count = query_count // query_block
    state = (
        jnp.full((block_count, heads_here, query_block), mask_value, jnp.float32),
        jnp.zeros((block_count, heads_here, query_block), jnp.float32),
        jnp.zeros((block_count, heads_here, query_block, HEAD_DIM), jnp.float32),
    )
    key_all, value_all = (
        lax.all_to_all(to_copies(key[0], parts), "seq", split_axis=0, concat_axis=0, tiled=True),
        lax.all_to_all(
            to_copies(blended_values, parts), "seq", split_axis=0, concat_axis=0, tiled=True
        ),
    )
    key_seg = segment_of(jnp.arange(n_seq * rows, dtype=jnp.int32), lengths)
    state = block_update(
        state,
        queries_here,
        query_seg,
        key_all.reshape(-1, heads_here, HEAD_DIM),
        value_all.reshape(-1, heads_here, HEAD_DIM),
        key_seg,
    )
    largest, totals, accum = state
    outcome = accum / totals[:, :, :, None]
    outcome = (
        outcome.transpose(0, 2, 1, 3)
        .reshape(query_count, heads_here * HEAD_DIM)
        .astype(jnp.bfloat16)
    )
    returned = lax.all_to_all(
        outcome.reshape(n_seq, sub_rows, heads_here * HEAD_DIM),
        "seq",
        split_axis=0,
        concat_axis=0,
        tiled=True,
    )
    width = width_all // HEAD_GROUPS
    restored = (
        returned.reshape(parts, HEAD_GROUPS, sub_rows, width)
        .transpose(0, 2, 1, 3)
        .reshape(rows, width_all)
    )
    return restored[None]


def solution(mesh):
    in_specs = (
        P("dp", "seq", None),
        P("dp", None, None),
        P("dp", None, None),
        P("dp", "seq", None),
        P("dp", "seq", None),
        P("dp", "seq", None),
        P(),
        P(),
        P("dp", "seq", None),
        P("dp", "seq", None),
        P("dp", None),
    )
    out_specs = P("dp", "seq", None)
    return jax.shard_map(body, mesh=mesh, in_specs=in_specs, out_specs=out_specs, check_vma=False)
```

profile of v0, /device:TPU:480, one launch (start us, length us, event | category | flops | bytes accessed | tf_op | source)
XLA Modules:
  0.0 302.0 jit_solution(16767233049610267462)
XLA Ops:
  2.5 7.3 %all-to-all-start = ((bf16[32,32,384]{2,1,0:T(8,128)(2,1)}), bf16[32,32,384]{2,1,0:T(8,128)(2,1)S(1)}, u32[]{:S(2)}, u32[]{:S(2)}) async-start(bf16[32,32,384]{2,1,0:T(8,128)(2,1)} %bitcast.5), calls=%async_computation | async-start | bytes 1572864 | tf_op jit(solution)/shard_map/all_to_all | solution.py:131
  16.7 7.0 %all-to-all-done = bf16[32,32,384]{2,1,0:T(8,128)(2,1)S(1)} async-done(((bf16[32,32,384]{2,1,0:T(8,128)(2,1)}), bf16[32,32,384]{2,1,0:T(8,128)(2,1)S(1)}, u32[]{:S(2)}, u32[]{:S(2)}) %all-to-all-start) | async-done | bytes 786464 | tf_op jit(solution)/shard_map/all_to_all | solution.py:131
  23.7 2.5 broadcast_in_dim.22
  26.2 4.9 %all-to-all-start.2 = ((bf16[32,128,384]{1,2,0:T(8,128)(2,1)}), bf16[32,128,384]{1,2,0:T(8,128)(2,1)}, u32[]{:S(2)}, u32[]{:S(2)}) async-start(bf16[32,128,384]{1,2,0:T(8,128)(2,1)} %bitcast.113), calls=%async_computation.2 | async-start | bytes 6291456 | tf_op jit(solution)/shard_map/all_to_all | solution.py:151
  31.9 39.4 %all-to-all-done.2 = bf16[32,128,384]{1,2,0:T(8,128)(2,1)} async-done(((bf16[32,128,384]{1,2,0:T(8,128)(2,1)}), bf16[32,128,384]{1,2,0:T(8,128)(2,1)}, u32[]{:S(2)}, u32[]{:S(2)}) %all-to-all-start.2) | async-done | bytes 3145760 | tf_op jit(solution)/shard_map/all_to_all | solution.py:151
  71.2 2.5 broadcast_in_dim.20
  73.7 5.0 %all-to-all-start.1 = ((bf16[32,128,384]{1,2,0:T(8,128)(2,1)}), bf16[32,128,384]{1,2,0:T(8,128)(2,1)}, u32[]{:S(2)}, u32[]{:S(2)}) async-start(bf16[32,128,384]{1,2,0:T(8,128)(2,1)} %bitcast.112), calls=%async_computation.1 | async-start | bytes 6291456 | tf_op jit(solution)/shard_map/all_to_all | solution.py:150
  79.6 5.5 %copy.58 = bf16[32,128,384]{1,0,2:T(8,128)(2,1)} copy(bf16[32,128,384]{1,2,0:T(8,128)(2,1)} %all-to-all-done.2) | data formatting | bytes 6291456 | tf_op jit(solution)/shard_map/all_to_all | solution.py:151
  85.1 6.0 %reshape_reshape.11 = bf16[8,512,3,128]{1,0,3,2:T(8,128)(2,1)} reshape(bf16[32,128,384]{1,0,2:T(8,128)(2,1)} %copy.58) | data formatting | bytes 6291456 | tf_op jit(solution)/shard_map/reshape;reshape | solution.py:47
  91.1 5.0 %copy.61 = bf16[8,512,3,128]{3,1,2,0:T(8,128)(2,1)} copy(bf16[8,512,3,128]{1,0,3,2:T(8,128)(2,1)} %reshape_reshape.11) | data formatting | bytes 6291456 | tf_op jit(solution)/shard_map/while | solution.py:81
  96.1 22.5 %all-to-all-done.1 = bf16[32,128,384]{1,2,0:T(8,128)(2,1)} async-done(((bf16[32,128,384]{1,2,0:T(8,128)(2,1)}), bf16[32,128,384]{1,2,0:T(8,128)(2,1)}, u32[]{:S(2)}, u32[]{:S(2)}) %all-to-all-start.1) | async-done | bytes 3145760 | tf_op jit(solution)/shard_map/all_to_all | solution.py:150
  118.5 5.6 %copy.55 = bf16[32,128,384]{1,0,2:T(8,128)(2,1)} copy(bf16[32,128,384]{1,2,0:T(8,128)(2,1)} %all-to-all-done.1) | data formatting | bytes 6291456 | tf_op jit(solution)/shard_map/all_to_all | solution.py:150
  124.1 6.0 %reshape_reshape.10 = bf16[8,512,3,128]{1,0,3,2:T(8,128)(2,1)} reshape(bf16[32,128,384]{1,0,2:T(8,128)(2,1)} %copy.55) | data formatting | bytes 6291456 | tf_op jit(solution)/shard_map/reshape;reshape | solution.py:46
  130.1 4.9 %copy.60 = bf16[8,512,3,128]{3,1,2,0:T(8,128)(2,1)} copy(bf16[8,512,3,128]{1,0,3,2:T(8,128)(2,1)} %reshape_reshape.10) | data formatting | bytes 6291456 | tf_op jit(solution)/shard_map/while | solution.py:81
  135.0 143.8 %while.28 = (s32[]{:T(128)}, f32[2,3,512]{2,1,0:T(4,128)S(1)}, f32[2,3,512,128]{3,2,1,0:T(8,128)}, bf16[2,512,3,128]{3,1,2,0:T(8,128)(2,1)S(1)}, s32[2,512]{1,0:...) while((s32[]{:T(128)}, f32[2,3,512]{2,1,0:T(4,128)S(1)}, ...), condition=%wide.region_12.13_spmd, body=%wide.region_7.12_spmd.sunk | while | flops 412163584 | bytes 28309368 | solution.py:81
  135.1 70.8 %while.29 = (s32[]{:T(128)}, f32[3,512]{1,0:T(4,128)S(1)}, f32[3,512]{1,0:T(4,128)S(1)}, f32[3,512,128]{2,1,0:T(8,128)S(1)}, s32[512]{0:T(512)S(1)}, /*index=5*/...) while((s32[]{:T(128)}, f32[3,512]{1,0:T(4,128)S(1)}, ...), condition=%wide.region_11.11_spmd.clone, body=%wide.region_8.10_spmd.clone.sunk | while | flops 412163584 | bytes 25928856 | solution.py:76
  135.4 3.4 %fusion.56 = (f32[3,512]{1,0:T(4,128)S(1)}, f32[3,512,512]{2,1,0:T(8,128)}) fusion(pred[512,512]{0,1:T(8,128)(4,1)S(1)} %broadcast_compare_fusion.2, bf16[512,3,128]{2,0,1:T(8,128)(2,1)S(1)} %get-tuple-element.362, bf16[8,512,3,128]{3,1,2,0:T(8,128)(2,1)} %get-tuple-element.361, s32[]{:T(128)} %get-tuple-element.344), kind=kOutput, calls=%fused_computation.4.clone.1 | convolution fusion | flops 203684352 | bytes 4200960 | tf_op jit(solution)/shard_map/while/body/eval_jaxpr/while/body/eval_jaxpr/qhd,khd->hqk/dot_general | solution.py:58
  138.8 2.8 fusion.57
  141.6 2.4 fusion.59
  144.2 3.4 %fusion.56 = (f32[3,512]{1,0:T(4,128)S(1)}, f32[3,512,512]{2,1,0:T(8,128)}) fusion(pred[512,512]{0,1:T(8,128)(4,1)S(1)} %broadcast_compare_fusion.2, bf16[512,3,128]{2,0,1:T(8,128)(2,1)S(1)} %get-tuple-element.362, bf16[8,512,3,128]{3,1,2,0:T(8,128)(2,1)} %get-tuple-element.361, s32[]{:T(128)} %get-tuple-element.344), kind=kOutput, calls=%fused_computation.4.clone.1 | convolution fusion | flops 203684352 | bytes 4200960 | tf_op jit(solution)/shard_map/while/body/eval_jaxpr/while/body/eval_jaxpr/qhd,khd->hqk/dot_general | solution.py:58
  147.6 2.8 fusion.57
  150.5 2.4 fusion.59
  153.1 3.4 %fusion.56 = (f32[3,512]{1,0:T(4,128)S(1)}, f32[3,512,512]{2,1,0:T(8,128)}) fusion(pred[512,512]{0,1:T(8,128)(4,1)S(1)} %broadcast_compare_fusion.2, bf16[512,3,128]{2,0,1:T(8,128)(2,1)S(1)} %get-tuple-element.362, bf16[8,512,3,128]{3,1,2,0:T(8,128)(2,1)} %get-tuple-element.361, s32[]{:T(128)} %get-tuple-element.344), kind=kOutput, calls=%fused_computation.4.clone.1 | convolution fusion | flops 203684352 | bytes 4200960 | tf_op jit(solution)/shard_map/while/body/eval_jaxpr/while/body/eval_jaxpr/qhd,khd->hqk/dot_general | solution.py:58
  156.5 2.8 fusion.57
  159.3 2.4 fusion.59
  161.9 3.4 %fusion.56 = (f32[3,512]{1,0:T(4,128)S(1)}, f32[3,512,512]{2,1,0:T(8,128)}) fusion(pred[512,512]{0,1:T(8,128)(4,1)S(1)} %broadcast_compare_fusion.2, bf16[512,3,128]{2,0,1:T(8,128)(2,1)S(1)} %get-tuple-element.362, bf16[8,512,3,128]{3,1,2,0:T(8,128)(2,1)} %get-tuple-element.361, s32[]{:T(128)} %get-tuple-element.344), kind=kOutput, calls=%fused_computation.4.clone.1 | convolution fusion | flops 203684352 | bytes 4200960 | tf_op jit(solution)/shard_map/while/body/eval_jaxpr/while/body/eval_jaxpr/qhd,khd->hqk/dot_general | solution.py:58
  165.3 2.8 fusion.57
  168.2 2.4 fusion.59
  170.8 3.4 %fusion.56 = (f32[3,512]{1,0:T(4,128)S(1)}, f32[3,512,512]{2,1,0:T(8,128)}) fusion(pred[512,512]{0,1:T(8,128)(4,1)S(1)} %broadcast_compare_fusion.2, bf16[512,3,128]{2,0,1:T(8,128)(2,1)S(1)} %get-tuple-element.362, bf16[8,512,3,128]{3,1,2,0:T(8,128)(2,1)} %get-tuple-element.361, s32[]{:T(128)} %get-tuple-element.344), kind=kOutput, calls=%fused_computation.4.clone.1 | convolution fusion | flops 203684352 | bytes 4200960 | tf_op jit(solution)/shard_map/while/body/eval_jaxpr/while/body/eval_jaxpr/qhd,khd->hqk/dot_general | solution.py:58
  174.2 2.8 fusion.57
  177.0 2.4 fusion.59
  179.6 3.4 %fusion.56 = (f32[3,512]{1,0:T(4,128)S(1)}, f32[3,512,512]{2,1,0:T(8,128)}) fusion(pred[512,512]{0,1:T(8,128)(4,1)S(1)} %broadcast_compare_fusion.2, bf16[512,3,128]{2,0,1:T(8,128)(2,1)S(1)} %get-tuple-element.362, bf16[8,512,3,128]{3,1,2,0:T(8,128)(2,1)} %get-tuple-element.361, s32[]{:T(128)} %get-tuple-element.344), kind=kOutput, calls=%fused_computation.4.clone.1 | convolution fusion | flops 203684352 | bytes 4200960 | tf_op jit(solution)/shard_map/while/body/eval_jaxpr/while/body/eval_jaxpr/qhd,khd->hqk/dot_general | solution.py:58
  183.1 2.8 fusion.57
  185.9 2.4 fusion.59
  188.5 3.4 %fusion.56 = (f32[3,512]{1,0:T(4,128)S(1)}, f32[3,512,512]{2,1,0:T(8,128)}) fusion(pred[512,512]{0,1:T(8,128)(4,1)S(1)} %broadcast_compare_fusion.2, bf16[512,3,128]{2,0,1:T(8,128)(2,1)S(1)} %get-tuple-element.362, bf16[8,512,3,128]{3,1,2,0:T(8,128)(2,1)} %get-tuple-element.361, s32[]{:T(128)} %get-tuple-element.344), kind=kOutput, calls=%fused_computation.4.clone.1 | convolution fusion | flops 203684352 | bytes 4200960 | tf_op jit(solution)/shard_map/while/body/eval_jaxpr/while/body/eval_jaxpr/qhd,khd->hqk/dot_general | solution.py:58
  191.9 2.8 fusion.57
  194.7 2.4 fusion.59
  197.4 3.4 %fusion.56 = (f32[3,512]{1,0:T(4,128)S(1)}, f32[3,512,512]{2,1,0:T(8,128)}) fusion(pred[512,512]{0,1:T(8,128)(4,1)S(1)} %broadcast_compare_fusion.2, bf16[512,3,128]{2,0,1:T(8,128)(2,1)S(1)} %get-tuple-element.362, bf16[8,512,3,128]{3,1,2,0:T(8,128)(2,1)} %get-tuple-element.361, s32[]{:T(128)} %get-tuple-element.344), kind=kOutput, calls=%fused_computation.4.clone.1 | convolution fusion | flops 203684352 | bytes 4200960 | tf_op jit(solution)/shard_map/while/body/eval_jaxpr/while/body/eval_jaxpr/qhd,khd->hqk/dot_general | solution.py:58
  200.8 2.8 fusion.57
  203.6 2.4 fusion.59
  207.0 70.8 %while.29 = (s32[]{:T(128)}, f32[3,512]{1,0:T(4,128)S(1)}, f32[3,512]{1,0:T(4,128)S(1)}, f32[3,512,128]{2,1,0:T(8,128)S(1)}, s32[512]{0:T(512)S(1)}, /*index=5*/...) while((s32[]{:T(128)}, f32[3,512]{1,0:T(4,128)S(1)}, ...), condition=%wide.region_11.11_spmd.clone, body=%wide.region_8.10_spmd.clone.sunk | while | flops 412163584 | bytes 25928856 | solution.py:76
  207.3 3.4 %fusion.56 = (f32[3,512]{1,0:T(4,128)S(1)}, f32[3,512,512]{2,1,0:T(8,128)}) fusion(pred[512,512]{0,1:T(8,128)(4,1)S(1)} %broadcast_compare_fusion.2, bf16[512,3,128]{2,0,1:T(8,128)(2,1)S(1)} %get-tuple-element.362, bf16[8,512,3,128]{3,1,2,0:T(8,128)(2,1)} %get-tuple-element.361, s32[]{:T(128)} %get-tuple-element.344), kind=kOutput, calls=%fused_computation.4.clone.1 | convolution fusion | flops 203684352 | bytes 4200960 | tf_op jit(solution)/shard_map/while/body/eval_jaxpr/while/body/eval_jaxpr/qhd,khd->hqk/dot_general | solution.py:58
  210.7 2.8 fusion.57
  213.5 2.4 fusion.59
  216.1 3.4 %fusion.56 = (f32[3,512]{1,0:T(4,128)S(1)}, f32[3,512,512]{2,1,0:T(8,128)}) fusion(pred[512,512]{0,1:T(8,128)(4,1)S(1)} %broadcast_compare_fusion.2, bf16[512,3,128]{2,0,1:T(8,128)(2,1)S(1)} %get-tuple-element.362, bf16[8,512,3,128]{3,1,2,0:T(8,128)(2,1)} %get-tuple-element.361, s32[]{:T(128)} %get-tuple-element.344), kind=kOutput, calls=%fused_computation.4.clone.1 | convolution fusion | flops 203684352 | bytes 4200960 | tf_op jit(solution)/shard_map/while/body/eval_jaxpr/while/body/eval_jaxpr/qhd,khd->hqk/dot_general | solution.py:58
  219.5 2.8 fusion.57
  222.4 2.4 fusion.59
  225.0 3.4 %fusion.56 = (f32[3,512]{1,0:T(4,128)S(1)}, f32[3,512,512]{2,1,0:T(8,128)}) fusion(pred[512,512]{0,1:T(8,128)(4,1)S(1)} %broadcast_compare_fusion.2, bf16[512,3,128]{2,0,1:T(8,128)(2,1)S(1)} %get-tuple-element.362, bf16[8,512,3,128]{3,1,2,0:T(8,128)(2,1)} %get-tuple-element.361, s32[]{:T(128)} %get-tuple-element.344), kind=kOutput, calls=%fused_computation.4.clone.1 | convolution fusion | flops 203684352 | bytes 4200960 | tf_op jit(solution)/shard_map/while/body/eval_jaxpr/while/body/eval_jaxpr/qhd,khd->hqk/dot_general | solution.py:58
  228.4 2.8 fusion.57
  231.2 2.4 fusion.59
  233.8 3.4 %fusion.56 = (f32[3,512]{1,0:T(4,128)S(1)}, f32[3,512,512]{2,1,0:T(8,128)}) fusion(pred[512,512]{0,1:T(8,128)(4,1)S(1)} %broadcast_compare_fusion.2, bf16[512,3,128]{2,0,1:T(8,128)(2,1)S(1)} %get-tuple-element.362, bf16[8,512,3,128]{3,1,2,0:T(8,128)(2,1)} %get-tuple-element.361, s32[]{:T(128)} %get-tuple-element.344), kind=kOutput, calls=%fused_computation.4.clone.1 | convolution fusion | flops 203684352 | bytes 4200960 | tf_op jit(solution)/shard_map/while/body/eval_jaxpr/while/body/eval_jaxpr/qhd,khd->hqk/dot_general | solution.py:58
  237.3 2.8 fusion.57
  240.1 2.4 fusion.59
  242.7 3.4 %fusion.56 = (f32[3,512]{1,0:T(4,128)S(1)}, f32[3,512,512]{2,1,0:T(8,128)}) fusion(pred[512,512]{0,1:T(8,128)(4,1)S(1)} %broadcast_compare_fusion.2, bf16[512,3,128]{2,0,1:T(8,128)(2,1)S(1)} %get-tuple-element.362, bf16[8,512,3,128]{3,1,2,0:T(8,128)(2,1)} %get-tuple-element.361, s32[]{:T(128)} %get-tuple-element.344), kind=kOutput, calls=%fused_computation.4.clone.1 | convolution fusion | flops 203684352 | bytes 4200960 | tf_op jit(solution)/shard_map/while/body/eval_jaxpr/while/body/eval_jaxpr/qhd,khd->hqk/dot_general | solution.py:58
  246.1 2.8 fusion.57
  248.9 2.4 fusion.59
  251.6 3.4 %fusion.56 = (f32[3,512]{1,0:T(4,128)S(1)}, f32[3,512,512]{2,1,0:T(8,128)}) fusion(pred[512,512]{0,1:T(8,128)(4,1)S(1)} %broadcast_compare_fusion.2, bf16[512,3,128]{2,0,1:T(8,128)(2,1)S(1)} %get-tuple-element.362, bf16[8,512,3,128]{3,1,2,0:T(8,128)(2,1)} %get-tuple-element.361, s32[]{:T(128)} %get-tuple-element.344), kind=kOutput, calls=%fused_computation.4.clone.1 | convolution fusion | flops 203684352 | bytes 4200960 | tf_op jit(solution)/shard_map/while/body/eval_jaxpr/while/body/eval_jaxpr/qhd,khd->hqk/dot_general | solution.py:58
  255.0 2.8 fusion.57
  260.4 3.4 %fusion.56 = (f32[3,512]{1,0:T(4,128)S(1)}, f32[3,512,512]{2,1,0:T(8,128)}) fusion(pred[512,512]{0,1:T(8,128)(4,1)S(1)} %broadcast_compare_fusion.2, bf16[512,3,128]{2,0,1:T(8,128)(2,1)S(1)} %get-tuple-element.362, bf16[8,512,3,128]{3,1,2,0:T(8,128)(2,1)} %get-tuple-element.361, s32[]{:T(128)} %get-tuple-element.344), kind=kOutput, calls=%fused_computation.4.clone.1 | convolution fusion | flops 203684352 | bytes 4200960 | tf_op jit(solution)/shard_map/while/body/eval_jaxpr/while/body/eval_jaxpr/qhd,khd->hqk/dot_general | solution.py:58
  263.8 2.8 fusion.57
  269.3 3.4 %fusion.56 = (f32[3,512]{1,0:T(4,128)S(1)}, f32[3,512,512]{2,1,0:T(8,128)}) fusion(pred[512,512]{0,1:T(8,128)(4,1)S(1)} %broadcast_compare_fusion.2, bf16[512,3,128]{2,0,1:T(8,128)(2,1)S(1)} %get-tuple-element.362, bf16[8,512,3,128]{3,1,2,0:T(8,128)(2,1)} %get-tuple-element.361, s32[]{:T(128)} %get-tuple-element.344), kind=kOutput, calls=%fused_computation.4.clone.1 | convolution fusion | flops 203684352 | bytes 4200960 | tf_op jit(solution)/shard_map/while/body/eval_jaxpr/while/body/eval_jaxpr/qhd,khd->hqk/dot_general | solution.py:58
  272.7 2.8 fusion.57
  275.5 2.4 fusion.59
  282.1 18.3 %all_to_all.20 = bf16[32,32,384]{2,1,0:T(8,128)(2,1)S(1)} all-to-all(bf16[32,32,384]{2,1,0:T(8,128)(2,1)S(1)} %convert_element_type.57), channel_id=1, replica_groups=mesh['dp'=16,'seq'=32] {'seq'}, dimensions={0} | all-to-all | bytes 1572864 | tf_op jit(solution)/shard_map/all_to_all | solution.py:171
  (183 shorter events, 26.7 us)
Async XLA Ops:
  0.0 14.5 %copy-start = (bf16[128,3072]{1,0:T(8,128)(2,1)S(1)}, bf16[128,3072]{1,0:T(8,128)(2,1)}, u32[]{:S(2)}) copy-start(bf16[128,3072]{1,0:T(8,128)(2,1)} %param.22) | copy-start | bytes 2359300
  0.0 9.8 %copy-start.9 = (s32[1,3]{1,0:T(1,128)S(1)}, s32[1,3]{1,0:T(1,128)}, u32[]{:S(2)}) copy-start(s32[1,3]{1,0:T(1,128)} %param.25) | copy-start | bytes 40
  0.0 10.0 %copy-start.2 = (bf16[1,128,3072]{2,1,0:T(8,128)(2,1)S(1)}, bf16[1,128,3072]{2,1,0:T(8,128)(2,1)}, u32[]{:S(2)}) copy-start(bf16[1,128,3072]{2,1,0:T(8,128)(2,1)} %param.15) | copy-start | bytes 2359300
  1.4 9.2 %copy-start.6 = (f32[1,128,2]{1,2,0:T(2,128)S(1)}, f32[1,128,2]{1,2,0:T(2,128)}, u32[]{:S(2)}) copy-start(f32[1,128,2]{1,2,0:T(2,128)} %param.24) | copy-start | bytes 3076
  1.4 9.2 %copy-start.7 = (s32[1,128,2]{1,2,0:T(2,128)S(1)}, s32[1,128,2]{1,2,0:T(2,128)}, u32[]{:S(2)}) copy-start(s32[1,128,2]{1,2,0:T(2,128)} %param.23) | copy-start | bytes 3076
  1.4 9.4 %copy-start.8 = (bf16[1,3,3072]{2,1,0:T(4,128)(2,1)S(1)}, bf16[1,3,3072]{2,1,0:T(4,128)(2,1)}, u32[]{:S(2)}) copy-start(bf16[1,3,3072]{2,1,0:T(4,128)(2,1)} %param.17) | copy-start | bytes 55300
  2.5 21.2 %all-to-all-start = ((bf16[32,32,384]{2,1,0:T(8,128)(2,1)}), bf16[32,32,384]{2,1,0:T(8,128)(2,1)S(1)}, u32[]{:S(2)}, u32[]{:S(2)}) async-start(bf16[32,32,384]{2,1,0:T(8,128)(2,1)} %bitcast.5), calls=%async_computation | async-start | bytes 1572864 | tf_op jit(solution)/shard_map/all_to_all | solution.py:131
  10.8 1.6 copy-start.4
  10.9 1.6 copy-start.5
  26.2 5.0 %copy-start.3 = (bf16[1,128,3072]{2,1,0:T(8,128)(2,1)S(1)}, bf16[1,128,3072]{2,1,0:T(8,128)(2,1)}, u32[]{:S(2)}) copy-start(bf16[1,128,3072]{2,1,0:T(8,128)(2,1)} %param.19) | copy-start | bytes 2359300
  26.2 45.0 %all-to-all-start.2 = ((bf16[32,128,384]{1,2,0:T(8,128)(2,1)}), bf16[32,128,384]{1,2,0:T(8,128)(2,1)}, u32[]{:S(2)}, u32[]{:S(2)}) async-start(bf16[32,128,384]{1,2,0:T(8,128)(2,1)} %bitcast.113), calls=%async_computation.2 | async-start | bytes 6291456 | tf_op jit(solution)/shard_map/all_to_all | solution.py:151
  73.7 44.8 %all-to-all-start.1 = ((bf16[32,128,384]{1,2,0:T(8,128)(2,1)}), bf16[32,128,384]{1,2,0:T(8,128)(2,1)}, u32[]{:S(2)}, u32[]{:S(2)}) async-start(bf16[32,128,384]{1,2,0:T(8,128)(2,1)} %bitcast.112), calls=%async_computation.1 | async-start | bytes 6291456 | tf_op jit(solution)/shard_map/all_to_all | solution.py:150
  138.8 2.8 copy-start.1
  147.6 2.8 copy-start.1
  156.5 2.8 copy-start.1
  165.3 2.8 copy-start.1
  174.2 2.8 copy-start.1
  183.0 2.8 copy-start.1
  191.9 2.8 copy-start.1
  200.8 2.8 copy-start.1
  210.7 2.8 copy-start.1
  219.5 2.8 copy-start.1
  228.4 2.8 copy-start.1
  237.2 2.8 copy-start.1
  246.1 2.8 copy-start.1
  255.0 2.8 copy-start.1
  263.8 2.8 copy-start.1
  272.7 2.8 copy-start.1
where the time goes:
time: 308 us; the launch traced here: 302 us
  matrix products  97.1 us (32%)
  waiting for transfers between devices  68.9 us (22%)
  other arithmetic  51.1 us (17%)
  local copies, waits for them, and re-layouts  48.1 us (16%)
  blocking collectives  18.3 us (6%)
  starting transfers between devices  17.3 us (6%)
    dot_general x16, matrix products, visit(): jnp.einsum('qhd,khd->hqk', query_tile, key_tile, preferred_element_type=j...  54.4 us
    reduce_sum x16, other arithmetic, visit(): new_total = old_total * rescale + jnp.sum(expo, axis=2)  44.3 us
    all_to_all x1, waiting for transfers between devices, body(): lax.all_to_all(to_copies(blended_values, parts), 'seq', split_axis=0, con...  39.4 us
    dot_general x16, matrix products, visit(): jnp.einsum('hqk,khd->hqd', expo.astype(jnp.bfloat16), value_tile, preferr...  37.6 us
    all_to_all x1, waiting for transfers between devices, body(): lax.all_to_all(to_copies(key[0], parts), 'seq', split_axis=0, concat_axis...  22.5 us
    all_to_all x1, blocking collectives, body(): lax.all_to_all(outcome.reshape(n_seq, sub_rows, heads_here * HEAD_DIM), '...  18.3 us
    while x3, local copies, waits for them, and re-layouts, block_update(): lax.map(per_query, (query_blocks, query_segs, largest, totals, accum))  10 us
    all_to_all x1, starting transfers between devices, body(): lax.all_to_all(to_groups(query[0], parts), 'seq', split_axis=0, concat_ax...  7.32 us
  transfers between devices with their start and end apart: 3, of which 3 were waited for; matrix products, arithmetic and copies ran while one was open for 8% of the time, Pallas kernels for 0%

commit v1 on v0

v1 whole, which is shorter than its diff:
```python
import functools
import math

import jax
import jax.numpy as jnp
from jax import lax
from jax.experimental import pallas as pl
from jax.experimental.pallas import tpu as pltpu
from jax.sharding import PartitionSpec as P

HEADS = 24
HEAD_DIM = 128
STYLE_ADAPTERS = 8
ADAPTER_RANK = 16
ROWS = 128
CHIPS = 16
PACK_TOKENS = 4096
BLOCKS = PACK_TOKENS // ROWS
HALF = ROWS // 2
Q_ROWS = ROWS + HALF
K_AT = Q_ROWS
V_AT = K_AT + 2 * ROWS
PIECE = V_AT + 2 * ROWS
KV_ROWS = 4 * ROWS
STEP = 8
TILE = 512

mask_value = -1e30
epsilon = 1e-06
to_base2 = math.log2(math.e) / math.sqrt(HEAD_DIM)


def heads_of(chip):
    trio = 3 * (chip // 2)
    if chip % 2 == 0:
        return trio, trio + 1, 0
    return trio + 2, trio + 1, HALF


def columns(head):
    return slice(head * HEAD_DIM, (head + 1) * HEAD_DIM)


def prepare_kernel(
    lengths, latents, shift, scale, query, key, value, down, up, index, weight, send,
    latents_in, query_in, key_in, value_in, down_in, up_in, stage, in_sems, out_sems,
):
    pairs = (
        (latents, latents_in),
        (down, down_in),
        (query, query_in),
        (key, key_in),
        (up, up_in),
        (value, value_in),
    )
    loads = [
        pltpu.make_async_copy(source, target, in_sems.at[n])
        for n, (source, target) in enumerate(pairs)
    ]
    for load in loads:
        load.start()
    first = lengths[0, 0]
    second = first + lengths[0, 1]
    start = lax.axis_index("seq") * ROWS
    positions = start + lax.broadcasted_iota(jnp.int32, (ROWS, 1), 0)
    adapter = lax.broadcasted_iota(jnp.int32, (ROWS, ROWS), 0) // ADAPTER_RANK
    coefficient = jnp.zeros((ROWS, ROWS), jnp.float32)
    for slot in range(index.shape[0]):
        coefficient += jnp.where(
            adapter == index[slot : slot + 1, :], weight[slot : slot + 1, :], 0.0
        )
    coefficient = coefficient.T

    def of_segment(table):
        rows = table[...].astype(jnp.float32)
        return jnp.where(
            positions < first, rows[0:1], jnp.where(positions < second, rows[1:2], rows[2:3])
        )

    loads[0].wait()
    floats = latents_in[...].astype(jnp.float32)
    center = jnp.mean(floats, axis=1, keepdims=True)
    spread = floats - center
    variance = jnp.mean(spread * spread, axis=1, keepdims=True)
    normed = spread * (1.0 / jnp.sqrt(variance + epsilon))
    modulated = ((1.0 + of_segment(scale)) * normed + of_segment(shift)).astype(jnp.bfloat16)
    loads[1].wait()
    low_rank = jnp.dot(modulated, down_in[...], preferred_element_type=jnp.float32)
    scaled = (low_rank * coefficient).astype(jnp.bfloat16)
    for load in loads[2:]:
        load.wait()
    sends = []
    for chip in range(CHIPS):
        main, shared, row = heads_of(chip)
        stage[chip, 0:ROWS] = query_in[:, columns(main)]
        stage[chip, ROWS:Q_ROWS] = query_in[row : row + HALF, columns(shared)]
        stage[chip, K_AT : K_AT + ROWS] = key_in[:, columns(main)]
        stage[chip, K_AT + ROWS : V_AT] = key_in[:, columns(shared)]
        for head, at in ((main, V_AT), (shared, V_AT + ROWS)):
            update = jnp.dot(scaled, up_in[:, columns(head)], preferred_element_type=jnp.float32)
            mixed = value_in[:, columns(head)].astype(jnp.float32) + update
            stage[chip, at : at + ROWS] = mixed.astype(jnp.bfloat16)
        copy = pltpu.make_async_copy(stage.at[chip], send.at[chip], out_sems.at[chip])
        copy.start()
        sends.append(copy)
    for copy in sends:
        copy.wait()


def attend_kernel(
    lengths, own, peer, out, main_queries, shared_queries, keys, values, sems
):
    own_blocks, peer_blocks = pl.ds(0, CHIPS), pl.ds(CHIPS, CHIPS)
    low_lanes = slice(0, HEAD_DIM)
    copies = []
    for slot in range(2):
        k_at, v_at = pl.ds(K_AT + slot * ROWS, ROWS), pl.ds(V_AT + slot * ROWS, ROWS)
        if slot == 0:
            pairs = [(own.at[:, 0:ROWS], main_queries.at[:, :, low_lanes])]
        else:
            pairs = [(own.at[:, ROWS:Q_ROWS], shared_queries.at[:, :, low_lanes])]
        for source, blocks in ((own, own_blocks), (peer, peer_blocks)):
            pairs.append((source.at[:, k_at], keys.at[slot, blocks, :, low_lanes]))
            pairs.append((source.at[:, v_at], values.at[slot, blocks, :, low_lanes]))
        group = [
            pltpu.make_async_copy(source, target, sems.at[slot * 5 + n])
            for n, (source, target) in enumerate(pairs)
        ]
        for copy in group:
            copy.start()
        copies.append(group)

    first = lengths[0, 0]
    second = first + lengths[0, 1]
    device = lax.axis_index("seq")
    core = lax.rem(device, 2)
    shared_row = lax.rem(lax.div(device, 2), 2) * HALF

    def segment_of(position):
        return (position >= first).astype(jnp.int32) + (position >= second).astype(jnp.int32)

    def query_features(source, first_row, rows):
        shape = (rows, HEAD_DIM)
        token = (2 * source + core) * ROWS + first_row
        segment = segment_of(token + lax.broadcasted_iota(jnp.int32, shape, 0))
        lane = lax.broadcasted_iota(jnp.int32, shape, 1)
        return jnp.where(lane == segment, 1.0, 0.0).astype(jnp.bfloat16)

    def key_features(token):
        shape = (ROWS, HEAD_DIM)
        segment = segment_of(token + lax.broadcasted_iota(jnp.int32, shape, 0))
        lane = lax.broadcasted_iota(jnp.int32, shape, 1)
        return jnp.where((lane == segment) | (lane >= 3), 0.0, mask_value).astype(jnp.bfloat16)

    ones = jnp.ones((ROWS, HEAD_DIM), jnp.bfloat16)

    def fill(source, _):
        main_queries[source, :, HEAD_DIM:] = query_features(source, 0, ROWS)
        shared_queries[source, :, HEAD_DIM:] = query_features(source, shared_row, HALF)
        for block, parity in ((source, core), (source + CHIPS, 1 - core)):
            features = key_features((2 * source + parity) * ROWS)
            for slot in range(2):
                keys[slot, block, :, HEAD_DIM:] = features
                values[slot, block, :, HEAD_DIM:] = ones
        return 0

    lax.fori_loop(0, CHIPS, fill, 0)

    def attend(slot, queries):
        def scores_of(step):
            tile = keys[slot, step * STEP : (step + 1) * STEP]
            return lax.dot_general(
                queries,
                tile.reshape(STEP * ROWS, 2 * HEAD_DIM),
                (((1,), (1,)), ((), ())),
                preferred_element_type=jnp.float32,
            )

        steps = BLOCKS // STEP
        scores = scores_of(0)
        largest = accum = None
        for step in range(steps):
            ahead = scores_of(step + 1) if step + 1 < steps else None
            top = jnp.max(scores, axis=1, keepdims=True)
            top = top if step == 0 else jnp.maximum(largest, top)
            expo = jnp.exp2((scores - top) * to_base2).astype(jnp.bfloat16)
            tile = values[slot, step * STEP : (step + 1) * STEP]
            part = jnp.dot(
                expo,
                tile.reshape(STEP * ROWS, 2 * HEAD_DIM),
                preferred_element_type=jnp.float32,
            )
            accum = part if step == 0 else accum * jnp.exp2((largest - top) * to_base2) + part
            largest, scores = top, ahead
        return (accum[:, 0:HEAD_DIM] / accum[:, HEAD_DIM:]).astype(jnp.bfloat16)

    for slot, queries, rows, lanes in (
        (0, main_queries, ROWS, slice(0, ROWS)),
        (1, shared_queries, HALF, slice(ROWS, Q_ROWS)),
    ):
        for copy in copies[slot]:
            copy.wait()
        sources = TILE // rows

        def visit(tile, _, slot=slot, queries=queries, rows=rows, lanes=lanes, sources=sources):
            at = pl.ds(tile * sources, sources)
            result = attend(slot, queries[at].reshape(TILE, 2 * HEAD_DIM))
            out[at, lanes] = result.reshape(sources, rows, HEAD_DIM)
            return 0

        lax.fori_loop(0, CHIPS // sources, visit, 0)


def restore_kernel(returned, out, sems):
    copies = []
    for chip in range(CHIPS):
        main, shared, row = heads_of(chip)
        for source, target in (
            (returned.at[chip, 0:ROWS], out.at[:, columns(main)]),
            (returned.at[chip, ROWS:Q_ROWS], out.at[row : row + HALF, columns(shared)]),
        ):
            copy = pltpu.make_async_copy(source, target, sems.at[len(copies)])
            copy.start()
            copies.append(copy)
    for copy in copies:
        copy.wait()


def body(
    latents,
    modulation_shift,
    modulation_scale,
    query,
    key,
    value,
    adapter_down_weight,
    adapter_up_weight,
    adapter_index,
    adapter_weight,
    sequence_length,
):
    same_core = [[2 * c + k for c in range(CHIPS)] for k in range(2)]
    vmem = pl.BlockSpec(memory_space=pltpu.VMEM)
    smem = pl.BlockSpec(memory_space=pltpu.SMEM)
    anywhere = pl.BlockSpec(memory_space=pl.ANY)
    params = pltpu.CompilerParams(vmem_limit_bytes=40 * 1024 * 1024)
    width = HEADS * HEAD_DIM
    wide, dma = jnp.bfloat16, pltpu.SemaphoreType.DMA

    send = pl.pallas_call(
        prepare_kernel,
        out_shape=jax.ShapeDtypeStruct((CHIPS, PIECE, HEAD_DIM), wide),
        in_specs=[smem, anywhere, vmem, vmem] + [anywhere] * 5 + [vmem, vmem],
        out_specs=anywhere,
        scratch_shapes=[
            pltpu.VMEM((ROWS, width), wide),
            pltpu.VMEM((ROWS, width), wide),
            pltpu.VMEM((ROWS, width), wide),
            pltpu.VMEM((ROWS, width), wide),
            pltpu.VMEM((width, ROWS), wide),
            pltpu.VMEM((ROWS, width), wide),
            pltpu.VMEM((CHIPS, PIECE, HEAD_DIM), wide),
            dma((6,)),
            dma((CHIPS,)),
        ],
        compiler_params=pltpu.CompilerParams(vmem_limit_bytes=60 * 1024 * 1024),
        name="prepare",
    )(
        sequence_length,
        latents[0],
        modulation_shift[0],
        modulation_scale[0],
        query[0],
        key[0],
        value[0],
        adapter_down_weight,
        adapter_up_weight,
        adapter_index[0].T,
        adapter_weight[0].T,
    )
    own = lax.all_to_all(
        send, "seq", split_axis=0, concat_axis=0, tiled=True, axis_index_groups=same_core
    )
    peer = lax.ppermute(own, "seq", [(d, d ^ 1) for d in range(2 * CHIPS)])
    attended = pl.pallas_call(
        attend_kernel,
        out_shape=jax.ShapeDtypeStruct((CHIPS, Q_ROWS, HEAD_DIM), wide),
        in_specs=[smem, vmem, vmem],
        out_specs=vmem,
        scratch_shapes=[
            pltpu.VMEM((CHIPS, ROWS, 2 * HEAD_DIM), wide),
            pltpu.VMEM((CHIPS, HALF, 2 * HEAD_DIM), wide),
            pltpu.VMEM((2, BLOCKS, ROWS, 2 * HEAD_DIM), wide),
            pltpu.VMEM((2, BLOCKS, ROWS, 2 * HEAD_DIM), wide),
            dma((10,)),
        ],
        compiler_params=params,
        name="attend",
    )(sequence_length, own, peer)
    returned = lax.all_to_all(
        attended, "seq", split_axis=0, concat_axis=0, tiled=True, axis_index_groups=same_core
    )
    restored = pl.pallas_call(
        restore_kernel,
        out_shape=jax.ShapeDtypeStruct((ROWS, width), wide),
        in_specs=[vmem],
        out_specs=anywhere,
        scratch_shapes=[dma((2 * CHIPS,))],
        compiler_params=params,
        name="restore",
    )(returned)
    return restored[None]


def solution(mesh):
    in_specs = (
        P("dp", "seq", None),
        P("dp", None, None),
        P("dp", None, None),
        P("dp", "seq", None),
        P("dp", "seq", None),
        P("dp", "seq", None),
        P(),
        P(),
        P("dp", "seq", None),
        P("dp", "seq", None),
        P("dp", None),
    )
    out_specs = P("dp", "seq", None)
    return jax.shard_map(body, mesh=mesh, in_specs=in_specs, out_specs=out_specs, check_vma=False)
```

time: 308 us -> 94.6 us (0.31); the launches traced: 302 us -> 94.3 us
  matrix products: 97.1 us -> 0 us
  waiting for transfers between devices: 68.9 us -> 5.25 us
  other arithmetic: 51.1 us -> 0 us
  local copies, waits for them, and re-layouts: 48.1 us -> 0.01 us
  blocking collectives: 18.3 us -> 61.9 us
  Pallas kernels: 0 us -> 25.2 us
  starting transfers between devices: 17.3 us -> 1.91 us
    dot_general x35 -> x0, matrix products: 97.1 us -> none  [the longest x16 54.4 us: visit(): jnp.einsum('qhd,khd->hqk', query_tile, key_tile, preferred_element_type=j...]
    all_to_all x3 -> x0, waiting for transfers between devices: 68.9 us -> none  [the longest x1 39.4 us: body(): lax.all_to_all(to_copies(blended_values, parts), 'seq', split_axis=0, con...]
    reduce_sum x22 -> x0, other arithmetic: 45.1 us -> none  [the longest x16 44.3 us: visit(): new_total = old_total * rescale + jnp.sum(expo, axis=2)]
    all_to_all x1 -> x2, blocking collectives: 18.3 us -> 61.9 us  [the longest x1 43.8 us: body(): lax.all_to_all(send, 'seq', split_axis=0, concat_axis=0, tiled=True, axis...]
    pallas_call x0 -> x3, Pallas kernels: none -> 25.2 us  [the longest x1 18.7 us: body(): pl.pallas_call(attend_kernel, out_shape=jax.ShapeDtypeStruct((CHIPS, Q_RO...]
    all_to_all x3 -> x0, starting transfers between devices: 17.3 us -> none  [the longest x1 7.32 us: body(): lax.all_to_all(to_groups(query[0], parts), 'seq', split_axis=0, concat_ax...]
    another operation x4 -> x0, local copies, waits for them, and re-layouts: 13.4 us -> none  [the longest x1 5.98 us: block_update(): value_rows.reshape(key_count // key_block, key_block, heads, depth)]
    all_to_all x2 -> x0, local copies, waits for them, and re-layouts: 11.2 us -> none  [the longest x1 5.61 us: body(): lax.all_to_all(to_copies(key[0], parts), 'seq', split_axis=0, concat_axis...]
  transfers between devices with their start and end apart: 3 -> 1, of which waited for: 3 -> 1; matrix products, arithmetic and copies ran while one was open for 8% -> 0% of each run, Pallas kernels for 0% -> 0%
where the time goes in v1:
time: 94.6 us; the launch traced here: 94.3 us
  blocking collectives  61.9 us (65%)
  Pallas kernels  25.2 us (27%)
  waiting for transfers between devices  5.25 us (6%)
  starting transfers between devices  1.91 us (2%)
    all_to_all x1, blocking collectives, body(): lax.all_to_all(send, 'seq', split_axis=0, concat_axis=0, tiled=True, axis...  43.8 us
    pallas_call x1, Pallas kernels, body(): pl.pallas_call(attend_kernel, out_shape=jax.ShapeDtypeStruct((CHIPS, Q_RO...  18.7 us
    all_to_all x1, blocking collectives, body(): lax.all_to_all(attended, 'seq', split_axis=0, concat_axis=0, tiled=True,...  18.1 us
    pallas_call x1, Pallas kernels, body(): pl.pallas_call(prepare_kernel, out_shape=jax.ShapeDtypeStruct((CHIPS, PIE...  5.41 us
    ppermute x1, waiting for transfers between devices, body(): peer = lax.ppermute(own, 'seq', [(d, d ^ 1) for d in range(2 * CHIPS)])  5.25 us
    ppermute x1, starting transfers between devices, body(): peer = lax.ppermute(own, 'seq', [(d, d ^ 1) for d in range(2 * CHIPS)])  1.91 us
  transfers between devices with their start and end apart: 1, of which 1 were waited for; matrix products, arithmetic and copies ran while one was open for 0% of the time, Pallas kernels for 0%

profile of v1, /device:TPU:480, one launch (start us, length us, event | category | flops | bytes accessed | tf_op | source)
XLA Modules:
  0.0 94.3 jit_solution(11329409625228552898)
XLA Ops:
  0.0 5.4 %prepare.1 = bf16[16,704,128]{2,1,0:T(8,128)(2,1)} custom-call(s32[1,3]{1,0:T(1,128)} %lengths.3, bf16[128,3072]{1,0:T(8,128)(2,1)} %bitcast.13, bf16[3,3072]{1,0:T(4,128)(2,1)} %bitcast.17, bf16[3,3072]{1,0:T(4,128)(2,1)} %bitcast.18, bf16[128,3072]{1,0:T(8,128)(2,1)} %bitcast.14, bf16[128,3072]{1,0:T(8,128)(2,1)} %bitcast.15, bf16[128,3072]{1,0:T(8,128)(2,1)} %bitcast.16, ...), custom_call_target="tpu_custom_call" | custom-call | tf_op jit(solution)/shard_map/prepare/pallas_call | solution.py:250
  5.4 0.0 copy-start
  5.4 43.8 %all_to_all.10.own = bf16[16,704,128]{2,1,0:T(8,128)(2,1)S(1)} all-to-all(bf16[16,704,128]{2,1,0:T(8,128)(2,1)} %prepare.1), channel_id=1, replica_groups={{0,2,4,6,8,10,12,14,16,18,20,22,24,26,28,30},{1,3,5,7,9,11,13,15,17,19,..., dimensions={0} | all-to-all | bytes 5767168 | tf_op jit(solution)/shard_map/all_to_all | solution.py:281
  49.3 1.9 %collective-permute-start = (bf16[16,704,128]{2,1,0:T(8,128)(2,1)S(1)}, bf16[16,704,128]{2,1,0:T(8,128)(2,1)S(1)}, u32[]{:S(2)}, u32[]{:S(2)}) collective-permute-start(bf16[16,704,128]{2,1,0:T(8,128)(2,1)S(1)} %all_to_all.10.own), channel_id=1, source_target_pairs={{0,1},{1,0},{2,3},{3,2},{4,5},{5,4},{6,7},{7,6},{8,9},{9,8},{10,11... | collective-permute-start | bytes 8650760 | tf_op jit(solution)/shard_map/ppermute | solution.py:284
  51.2 5.2 %collective-permute-done.peer = bf16[16,704,128]{2,1,0:T(8,128)(2,1)S(1)} collective-permute-done((bf16[16,704,128]{2,1,0:T(8,128)(2,1)S(1)}, bf16[16,704,128]{2,1,0:T(8,128)(2,1)S(1)}, u32[]{:S(2)}, u32[]{:S(2)}) %collective-permute-start) | collective-permute-done | bytes 2883616 | tf_op jit(solution)/shard_map/ppermute | solution.py:284
  56.4 0.0 copy-done
  56.4 18.7 %attend.1 = bf16[16,192,128]{2,1,0:T(8,128)(2,1)S(1)} custom-call(s32[1,3]{1,0:T(1,128)S(1)} %copy-done, bf16[16,704,128]{2,1,0:T(8,128)(2,1)S(1)} %all_to_all.10.own, bf16[16,704,128]{2,1,0:T(8,128)(2,1)S(1)} %collective-permute-done.peer), custom_call_target="tpu_custom_call" | custom-call | tf_op jit(solution)/shard_map/attend/pallas_call | solution.py:285
  75.1 18.1 %all_to_all.11.returned = bf16[16,192,128]{2,1,0:T(8,128)(2,1)S(1)} all-to-all(bf16[16,192,128]{2,1,0:T(8,128)(2,1)S(1)} %attend.1), channel_id=1, replica_groups={{0,2,4,6,8,10,12,14,16,18,20,22,24,26,28,30},{1,3,5,7,9,11,13,15,17,19,..., dimensions={0} | all-to-all | bytes 1572864 | tf_op jit(solution)/shard_map/all_to_all | solution.py:300
  93.2 1.1 %restore.1 = bf16[128,3072]{1,0:T(8,128)(2,1)} custom-call(bf16[16,192,128]{2,1,0:T(8,128)(2,1)S(1)} %all_to_all.11.returned), custom_call_target="tpu_custom_call" | custom-call | tf_op jit(solution)/shard_map/restore/pallas_call | solution.py:303
Async XLA Ops:
  5.4 51.0 %copy-start = (s32[1,3]{1,0:T(1,128)S(1)}, s32[1,3]{1,0:T(1,128)}, u32[]{:S(2)}) copy-start(s32[1,3]{1,0:T(1,128)} %lengths.3) | copy-start | bytes 40
  49.3 7.2 %collective-permute-start = (bf16[16,704,128]{2,1,0:T(8,128)(2,1)S(1)}, bf16[16,704,128]{2,1,0:T(8,128)(2,1)S(1)}, u32[]{:S(2)}, u32[]{:S(2)}) collective-permute-start(bf16[16,704,128]{2,1,0:T(8,128)(2,1)S(1)} %all_to_all.10.own), channel_id=1, source_target_pairs={{0,1},{1,0},{2,3},{3,2},{4,5},{5,4},{6,7},{7,6},{8,9},{9,8},{10,11... | collective-permute-start | bytes 8650760 | tf_op jit(solution)/shard_map/ppermute | solution.py:284

commit v2 on v1

v2 whole, which is shorter than its diff:
```python
import functools
import math

import jax
import jax.numpy as jnp
from jax import lax
from jax.experimental import pallas as pl
from jax.experimental.pallas import tpu as pltpu
from jax.sharding import PartitionSpec as P

HEADS = 24
HEAD_DIM = 128
STYLE_ADAPTERS = 8
ADAPTER_RANK = 16
ROWS = 128
CHIPS = 16
PACK_TOKENS = 4096
BLOCKS = PACK_TOKENS // ROWS
HALF = ROWS // 2
Q_ROWS = ROWS + HALF
K_AT = Q_ROWS
V_AT = K_AT + 2 * ROWS
PIECE = V_AT + 2 * ROWS
KV_ROWS = 4 * ROWS
TILE = 512
TILES = CHIPS * Q_ROWS // TILE
STEP = 8
SAFE_LOW, SAFE_HIGH = 2.0**-60, 2.0**100

mask_value = -1e30
epsilon = 1e-06
to_base2 = math.log2(math.e) / math.sqrt(HEAD_DIM)


def heads_of(chip):
    trio = 3 * (chip // 2)
    if chip % 2 == 0:
        return trio, trio + 1, 0
    return trio + 2, trio + 1, HALF


def columns(head):
    return slice(head * HEAD_DIM, (head + 1) * HEAD_DIM)


def prepare_kernel(
    lengths, latents, shift, scale, query, key, value, down, up, index, weight, send,
    latents_in, query_in, key_in, value_in, down_in, up_in, stage, in_sems, out_sems,
):
    pairs = (
        (latents, latents_in),
        (down, down_in),
        (up, up_in),
        (value, value_in),
        (query, query_in),
        (key, key_in),
    )
    loads = [
        pltpu.make_async_copy(source, target, in_sems.at[n])
        for n, (source, target) in enumerate(pairs)
    ]
    for load in loads:
        load.start()
    first = lengths[0, 0]
    second = first + lengths[0, 1]
    start = lax.axis_index("seq") * ROWS
    shape = (ROWS, ROWS)
    adapter = lax.broadcasted_iota(jnp.int32, shape, 0) // ADAPTER_RANK
    coefficient = jnp.zeros(shape, jnp.float32)
    for slot in range(index.shape[0]):
        coefficient += jnp.where(
            adapter == index[slot : slot + 1, :], weight[slot : slot + 1, :], 0.0
        )
    coefficient = coefficient.T
    segments = shift.shape[0]
    token = start + lax.broadcasted_iota(jnp.int32, (ROWS, segments), 0)
    segment = (token >= first).astype(jnp.int32) + (token >= second).astype(jnp.int32)
    lane = lax.broadcasted_iota(jnp.int32, (ROWS, segments), 1)
    chosen = jnp.where(lane == segment, 1.0, 0.0).astype(jnp.bfloat16)

    width = latents_in.shape[1]
    wide = 512
    chunks = width // wide

    def lanes_of(chunk):
        return slice(chunk * wide, (chunk + 1) * wide)

    def folded(values):
        parts = [values[:, n * HEAD_DIM : (n + 1) * HEAD_DIM] for n in range(wide // HEAD_DIM)]
        return functools.reduce(jnp.add, parts)

    loads[0].wait()
    zeros = jnp.zeros((ROWS, HEAD_DIM), jnp.float32)
    sums = zeros
    for n in range(chunks):
        sums += folded(latents_in[:, lanes_of(n)].astype(jnp.float32))
    center = jnp.sum(sums, axis=1, keepdims=True) * (1.0 / width)
    sums = zeros
    for n in range(chunks):
        spread = latents_in[:, lanes_of(n)].astype(jnp.float32) - center
        sums += folded(spread * spread)
    variance = jnp.sum(sums, axis=1, keepdims=True) * (1.0 / width)
    inverse = 1.0 / jnp.sqrt(variance + epsilon)
    loads[1].wait()
    low_rank = zeros
    for n in range(chunks):
        lanes = lanes_of(n)
        normed = (latents_in[:, lanes].astype(jnp.float32) - center) * inverse
        scales = jnp.dot(chosen, scale[:, lanes], preferred_element_type=jnp.float32)
        shifts = jnp.dot(chosen, shift[:, lanes], preferred_element_type=jnp.float32)
        modulated = ((1.0 + scales) * normed + shifts).astype(jnp.bfloat16)
        low_rank += jnp.dot(modulated, down_in[lanes, :], preferred_element_type=jnp.float32)
    scaled = (low_rank * coefficient).astype(jnp.bfloat16)
    for load in loads[2:]:
        load.wait()
    trio = 3 * HEAD_DIM

    def post(chip):
        return pltpu.make_async_copy(stage.at[chip], send.at[chip], out_sems.at[chip])

    for pair in range(CHIPS // 2):
        lanes = slice(pair * trio, (pair + 1) * trio)
        update = jnp.dot(scaled, up_in[:, lanes], preferred_element_type=jnp.float32)
        mixed = value_in[:, lanes].astype(jnp.float32) + update
        turned = [mixed[:, columns(head)].T.astype(jnp.bfloat16) for head in range(3)]
        for side in range(2):
            main, shared, row = heads_of(side)
            main_at, shared_at = columns(3 * pair + main), columns(3 * pair + shared)
            chip = 2 * pair + side
            stage[chip, 0:ROWS] = query_in[:, main_at]
            stage[chip, ROWS:Q_ROWS] = query_in[row : row + HALF, shared_at]
            stage[chip, K_AT : K_AT + ROWS] = key_in[:, main_at]
            stage[chip, K_AT + ROWS : V_AT] = key_in[:, shared_at]
            stage[chip, V_AT : V_AT + ROWS] = turned[main]
            stage[chip, V_AT + ROWS : PIECE] = turned[shared]
            post(chip).start()
    for chip in range(CHIPS):
        post(chip).wait()


def nt(left, right):
    return lax.dot_general(
        left, right, (((1,), (1,)), ((), ())), preferred_element_type=jnp.float32
    )


class Attention:
    def __init__(self, lengths):
        self.first = lengths[0, 0]
        self.second = self.first + lengths[0, 1]
        device = lax.axis_index("seq")
        self.core = lax.rem(device, 2)
        self.shared_row = lax.rem(lax.div(device, 2), 2) * HALF

    def same_segment_lane(self, source, core):
        shape = (ROWS, HEAD_DIM)
        token = (2 * source + core) * ROWS + lax.broadcasted_iota(jnp.int32, shape, 0)
        segment = (token >= self.first).astype(jnp.int32)
        segment += (token >= self.second).astype(jnp.int32)
        lane = lax.broadcasted_iota(jnp.int32, shape, 1)
        return lane == segment, lane

    def key_mark(self, source, core):
        same, lane = self.same_segment_lane(source, core)
        return jnp.where(same | (lane >= 3), 0.0, mask_value).astype(jnp.bfloat16)

    def fill(self, own, queries, query_mark, key_marks, peer_marks):
        low, high = slice(0, HEAD_DIM), slice(HEAD_DIM, 2 * HEAD_DIM)
        main, shared = TILE // ROWS, TILE // HALF

        def visit(source, _):
            same, _ = self.same_segment_lane(source, self.core)
            query_mark[...] = jnp.where(same, 1.0, 0.0).astype(jnp.bfloat16)
            key_marks[source] = self.key_mark(source, self.core)
            peer_marks[source] = self.key_mark(source, 1 - self.core)
            tile = lax.div(source, main)
            rows = pl.ds(pl.multiple_of(lax.rem(source, main) * ROWS, ROWS), ROWS)
            queries[tile, rows, low] = own[source, 0:ROWS]
            queries[tile, rows, high] = query_mark[...]
            tile = CHIPS // main + lax.div(source, shared)
            rows = pl.ds(pl.multiple_of(lax.rem(source, shared) * HALF, HALF), HALF)
            queries[tile, rows, low] = own[source, ROWS:Q_ROWS]
            mark_rows = pl.ds(pl.multiple_of(self.shared_row, HALF), HALF)
            queries[tile, rows, high] = query_mark[mark_rows, :]
            return 0

        lax.fori_loop(0, CHIPS, visit, 0)

    def rows_of(self, tile):
        kind = (tile >= CHIPS * ROWS // TILE).astype(jnp.int32)
        key_rows = pl.ds(pl.multiple_of(K_AT + kind * ROWS, HALF), ROWS)
        value_rows = pl.ds(pl.multiple_of(V_AT + kind * ROWS, HALF), ROWS)
        return key_rows, value_rows

    def add(self, tile, queries, source, marks, weights, total, accum):
        key_rows, value_rows = self.rows_of(tile)
        steps, count = CHIPS // STEP, STEP * ROWS
        for step in range(steps + 1):
            if step < steps:
                blocks = slice(step * STEP, (step + 1) * STEP)
                key_tile = source[blocks, key_rows].reshape(count, HEAD_DIM)
                mark = marks[blocks].reshape(count, HEAD_DIM)
                scores = nt(jnp.concatenate([key_tile, mark], axis=1), queries)
                expo = jnp.exp2(scores * to_base2)
                sums = jnp.sum(expo.reshape(count // 8, 8, TILE), axis=0)
                total = sums if total is None else total + sums
                weights[step % 2] = expo.astype(jnp.bfloat16)
            if step > 0:
                start = (step - 1) * STEP
                value_tile = [source[start + n, value_rows] for n in range(STEP)]
                part = jnp.dot(
                    jnp.concatenate(value_tile, axis=1),
                    weights[(step - 1) % 2],
                    preferred_element_type=jnp.float32,
                )
                accum = part if accum is None else accum + part
        return total, accum


def own_kernel(lengths, own, accums, totals, queries, peer_marks, query_mark, key_marks, weights):
    attention = Attention(lengths)
    attention.fill(own, queries, query_mark, key_marks, peer_marks)

    def visit(tile, _):
        total, accum = attention.add(tile, queries[tile], own, key_marks, weights, None, None)
        accums[tile] = accum
        totals[tile] = total
        return 0

    lax.fori_loop(0, TILES, visit, 0)


def peer_kernel(
    lengths, own, peer, accums, totals, queries, key_marks, out, weights,
    results, largest_ref, total_ref, accum_ref,
):
    attention = Attention(lengths)
    other = 1 - attention.core

    def store(tile, accum, total):
        results[tile] = (accum * (1.0 / total)).T.astype(jnp.bfloat16)

    def visit(tile, _):
        total, accum = attention.add(
            tile, queries[tile], peer, key_marks, weights, totals[tile], accums[tile]
        )
        total = jnp.sum(total, axis=0, keepdims=True)
        store(tile, accum, total)

        safe = (jnp.max(total) < SAFE_HIGH) & (jnp.min(total) > SAFE_LOW)

        @pl.when(jnp.logical_not(safe))
        def _():
            key_rows, value_rows = attention.rows_of(tile)
            largest_ref[...] = jnp.full((1, TILE), mask_value, jnp.float32)
            total_ref[...] = jnp.zeros((1, TILE), jnp.float32)
            accum_ref[...] = jnp.zeros((HEAD_DIM, TILE), jnp.float32)
            for source, core in ((own, attention.core), (peer, other)):

                def block(index, _, source=source, core=core):
                    mark = attention.key_mark(index, core)
                    key_tile = jnp.concatenate([source[index, key_rows], mark], axis=1)
                    scores = nt(key_tile, queries[tile])
                    largest = largest_ref[...]
                    top = jnp.maximum(largest, jnp.max(scores, axis=0, keepdims=True))
                    rescale = jnp.exp2((largest - top) * to_base2)
                    expo = jnp.exp2((scores - top) * to_base2)
                    largest_ref[...] = top
                    total_ref[...] = total_ref[...] * rescale + jnp.sum(
                        expo, axis=0, keepdims=True
                    )
                    accum_ref[...] = accum_ref[...] * rescale + jnp.dot(
                        source[index, value_rows],
                        expo.astype(jnp.bfloat16),
                        preferred_element_type=jnp.float32,
                    )
                    return 0

                lax.fori_loop(0, CHIPS, block, 0)
            store(tile, accum_ref[...], total_ref[...])

        return 0

    lax.fori_loop(0, TILES, visit, 0)
    main = CHIPS * ROWS // TILE
    out[:, 0:ROWS] = results[0:main].reshape(CHIPS, ROWS, HEAD_DIM)
    out[:, ROWS:Q_ROWS] = results[main:TILES].reshape(CHIPS, HALF, HEAD_DIM)


def restore_kernel(returned, out, sems):
    copies = []
    for chip in range(CHIPS):
        main, shared, row = heads_of(chip)
        for source, target in (
            (returned.at[chip, 0:ROWS], out.at[:, columns(main)]),
            (returned.at[chip, ROWS:Q_ROWS], out.at[row : row + HALF, columns(shared)]),
        ):
            copy = pltpu.make_async_copy(source, target, sems.at[len(copies)])
            copy.start()
            copies.append(copy)
    for copy in copies:
        copy.wait()


def body(
    latents,
    modulation_shift,
    modulation_scale,
    query,
    key,
    value,
    adapter_down_weight,
    adapter_up_weight,
    adapter_index,
    adapter_weight,
    sequence_length,
):
    same_core = [[2 * c + k for c in range(CHIPS)] for k in range(2)]
    vmem = pl.BlockSpec(memory_space=pltpu.VMEM)
    smem = pl.BlockSpec(memory_space=pltpu.SMEM)
    anywhere = pl.BlockSpec(memory_space=pl.ANY)
    params = pltpu.CompilerParams(vmem_limit_bytes=36 * 1024 * 1024)
    width = HEADS * HEAD_DIM
    wide, dma = jnp.bfloat16, pltpu.SemaphoreType.DMA

    send = pl.pallas_call(
        prepare_kernel,
        out_shape=jax.ShapeDtypeStruct((CHIPS, PIECE, HEAD_DIM), wide),
        in_specs=[smem, anywhere, vmem, vmem] + [anywhere] * 5 + [vmem, vmem],
        out_specs=anywhere,
        scratch_shapes=[
            pltpu.VMEM((ROWS, width), wide),
            pltpu.VMEM((ROWS, width), wide),
            pltpu.VMEM((ROWS, width), wide),
            pltpu.VMEM((ROWS, width), wide),
            pltpu.VMEM((width, ROWS), wide),
            pltpu.VMEM((ROWS, width), wide),
            pltpu.VMEM((CHIPS, PIECE, HEAD_DIM), wide),
            dma((6,)),
            dma((CHIPS,)),
        ],
        compiler_params=pltpu.CompilerParams(vmem_limit_bytes=60 * 1024 * 1024),
        name="prepare",
    )(
        sequence_length,
        latents[0],
        modulation_shift[0],
        modulation_scale[0],
        query[0],
        key[0],
        value[0],
        adapter_down_weight,
        adapter_up_weight,
        adapter_index[0].T,
        adapter_weight[0].T,
    )
    own = lax.all_to_all(
        send, "seq", split_axis=0, concat_axis=0, tiled=True, axis_index_groups=same_core
    )
    peer = lax.ppermute(own, "seq", [(d, d ^ 1) for d in range(2 * CHIPS)])
    pairs = TILES * TILE * PACK_TOKENS // 2
    cost = pl.CostEstimate(
        flops=6 * HEAD_DIM * pairs, bytes_accessed=4 << 20, transcendentals=pairs
    )
    marks = pltpu.VMEM((CHIPS, ROWS, HEAD_DIM), wide)
    weights = pltpu.VMEM((2, STEP * ROWS, TILE), wide)
    state = pl.pallas_call(
        own_kernel,
        out_shape=[
            jax.ShapeDtypeStruct((TILES, HEAD_DIM, TILE), jnp.float32),
            jax.ShapeDtypeStruct((TILES, 8, TILE), jnp.float32),
            jax.ShapeDtypeStruct((TILES, TILE, 2 * HEAD_DIM), wide),
            jax.ShapeDtypeStruct((CHIPS, ROWS, HEAD_DIM), wide),
        ],
        in_specs=[smem, vmem],
        out_specs=[vmem] * 4,
        scratch_shapes=[pltpu.VMEM((ROWS, HEAD_DIM), wide), marks, weights],
        compiler_params=params,
        cost_estimate=cost,
        name="attend_own",
    )(sequence_length, own)
    attended = pl.pallas_call(
        peer_kernel,
        out_shape=jax.ShapeDtypeStruct((CHIPS, Q_ROWS, HEAD_DIM), wide),
        in_specs=[smem] + [vmem] * 6,
        out_specs=vmem,
        scratch_shapes=[
            weights,
            pltpu.VMEM((TILES, TILE, HEAD_DIM), wide),
            pltpu.VMEM((1, TILE), jnp.float32),
            pltpu.VMEM((1, TILE), jnp.float32),
            pltpu.VMEM((HEAD_DIM, TILE), jnp.float32),
        ],
        compiler_params=params,
        cost_estimate=cost,
        name="attend_peer",
    )(sequence_length, own, peer, *state)
    returned = lax.all_to_all(
        attended, "seq", split_axis=0, concat_axis=0, tiled=True, axis_index_groups=same_core
    )
    restored = pl.pallas_call(
        restore_kernel,
        out_shape=jax.ShapeDtypeStruct((ROWS, width), wide),
        in_specs=[vmem],
        out_specs=anywhere,
        scratch_shapes=[dma((2 * CHIPS,))],
        compiler_params=params,
        name="restore",
    )(returned)
    return restored[None]


def solution(mesh):
    in_specs = (
        P("dp", "seq", None),
        P("dp", None, None),
        P("dp", None, None),
        P("dp", "seq", None),
        P("dp", "seq", None),
        P("dp", "seq", None),
        P(),
        P(),
        P("dp", "seq", None),
        P("dp", "seq", None),
        P("dp", None),
    )
    out_specs = P("dp", "seq", None)
    return jax.shard_map(body, mesh=mesh, in_specs=in_specs, out_specs=out_specs, check_vma=False)
```

time: 94.6 us -> 112 us (1.18)
  Pallas kernels: 25.2 us -> 50.7 us
  waiting for transfers between devices: 5.25 us -> 0.01 us
  blocking collectives: 61.9 us -> 58.8 us
    pallas_call x1 -> x2, Pallas kernels: 18.7 us -> 43.8 us  [the longest x1 36 us: body(): pl.pallas_call(peer_kernel, out_shape=jax.ShapeDtypeStruct((CHIPS, Q_ROWS...]
    ppermute x1, waiting for transfers between devices: 5.25 us -> 0.01 us  [body(): peer = lax.ppermute(own, 'seq', [(d, d ^ 1) for d in range(2 * CHIPS)])]
    all_to_all x1, blocking collectives: 18.1 us -> 15 us  [body(): lax.all_to_all(attended, 'seq', split_axis=0, concat_axis=0, tiled=True,...]
  transfers between devices with their start and end apart: 1 -> 1, of which waited for: 1 -> 0; matrix products, arithmetic and copies ran while one was open for 0% -> 0% of each run, Pallas kernels for 0% -> 7%
where the time goes in v2:
time: 112 us; the launch traced here: 111 us
  blocking collectives  58.8 us (52%)
  Pallas kernels  50.7 us (45%)
  starting transfers between devices  1.91 us (2%)
    all_to_all x1, blocking collectives, body(): lax.all_to_all(send, 'seq', split_axis=0, concat_axis=0, tiled=True, axis...  43.8 us
    pallas_call x1, Pallas kernels, body(): pl.pallas_call(peer_kernel, out_shape=jax.ShapeDtypeStruct((CHIPS, Q_ROWS...  36 us
    all_to_all x1, blocking collectives, body(): lax.all_to_all(attended, 'seq', split_axis=0, concat_axis=0, tiled=True,...  15 us
    pallas_call x1, Pallas kernels, body(): pl.pallas_call(own_kernel, out_shape=[jax.ShapeDtypeStruct((TILES, HEAD_D...  7.8 us
    pallas_call x1, Pallas kernels, body(): pl.pallas_call(prepare_kernel, out_shape=jax.ShapeDtypeStruct((CHIPS, PIE...  5.7 us
  transfers between devices with their start and end apart: 1, of which 0 were waited for; matrix products, arithmetic and copies ran while one was open for 0% of the time, Pallas kernels for 7%

profile of v2, /device:TPU:480, one launch (start us, length us, event | category | flops | bytes accessed | tf_op | source)
XLA Modules:
  0.0 111.4 jit_solution(15997871492118311894)
XLA Ops:
  0.0 5.7 %prepare.1 = bf16[16,704,128]{2,1,0:T(8,128)(2,1)} custom-call(s32[1,3]{1,0:T(1,128)} %lengths.5, bf16[128,3072]{1,0:T(8,128)(2,1)} %bitcast.13, bf16[3,3072]{1,0:T(4,128)(2,1)} %bitcast.17, bf16[3,3072]{1,0:T(4,128)(2,1)} %bitcast.18, bf16[128,3072]{1,0:T(8,128)(2,1)} %bitcast.14, bf16[128,3072]{1,0:T(8,128)(2,1)} %bitcast.15, bf16[128,3072]{1,0:T(8,128)(2,1)} %bitcast.16, ...), custom_call_target="tpu_custom_call" | custom-call | tf_op jit(solution)/shard_map/prepare/pallas_call | solution.py:326
  5.7 0.0 copy-start
  5.7 43.8 %all_to_all.10.own = bf16[16,704,128]{2,1,0:T(8,128)(2,1)S(1)} all-to-all(bf16[16,704,128]{2,1,0:T(8,128)(2,1)} %prepare.1), channel_id=1, replica_groups={{0,2,4,6,8,10,12,14,16,18,20,22,24,26,28,30},{1,3,5,7,9,11,13,15,17,19,..., dimensions={0} | all-to-all | bytes 5767168 | tf_op jit(solution)/shard_map/all_to_all | solution.py:357
  49.5 1.9 %collective-permute-start = (bf16[16,704,128]{2,1,0:T(8,128)(2,1)S(1)}, bf16[16,704,128]{2,1,0:T(8,128)(2,1)S(1)}, u32[]{:S(2)}, u32[]{:S(2)}) collective-permute-start(bf16[16,704,128]{2,1,0:T(8,128)(2,1)S(1)} %all_to_all.10.own), channel_id=1, source_target_pairs={{0,1},{1,0},{2,3},{3,2},{4,5},{5,4},{6,7},{7,6},{8,9},{9,8},{10,11... | collective-permute-start | bytes 8650760 | tf_op jit(solution)/shard_map/ppermute | solution.py:360
  51.5 0.0 copy-done
  51.5 7.8 %attend_own.1 = (f32[6,128,512]{2,1,0:T(8,128)S(1)}, f32[6,8,512]{2,1,0:T(8,128)S(1)}, bf16[6,512,256]{2,1,0:T(8,128)(2,1)S(1)}, bf16[16,128,128]{2,1,0:T(8,128)(2,1)S(1)}) custom-call(s32[1,3]{1,0:T(1,128)S(1)} %copy-done, bf16[16,704,128]{2,1,0:T(8,128)(2,1)S(1)} %all_to_all.10.own), custom_call_target="tpu_custom_call" | custom-call | flops 4831838208 | bytes 4194304 | tf_op jit(solution)/shard_map/attend_own/pallas_call | solution.py:367
  59.3 0.0 collective-permute-done.peer
  59.3 36.0 %attend_peer.1 = bf16[16,192,128]{2,1,0:T(8,128)(2,1)S(1)} custom-call(s32[1,3]{1,0:T(1,128)S(1)} %copy-done, bf16[16,704,128]{2,1,0:T(8,128)(2,1)S(1)} %all_to_all.10.own, bf16[16,704,128]{2,1,0:T(8,128)(2,1)S(1)} %collective-permute-done.peer, f32[6,128,512]{2,1,0:T(8,128)S(1)} %get-tuple-element.9.accums, f32[6,8,512]{2,1,0:T(8,128)S(1)} %get-tuple-element.10.totals, ...), custom_call_target="tpu_custom_call" | custom-call | flops 4831838208 | bytes 4194304 | tf_op jit(solution)/shard_map/attend_peer/pallas_call | solution.py:382
  95.3 15.0 %all_to_all.11.returned = bf16[16,192,128]{2,1,0:T(8,128)(2,1)S(1)} all-to-all(bf16[16,192,128]{2,1,0:T(8,128)(2,1)S(1)} %attend_peer.1), channel_id=1, replica_groups={{0,2,4,6,8,10,12,14,16,18,20,22,24,26,28,30},{1,3,5,7,9,11,13,15,17,19,..., dimensions={0} | all-to-all | bytes 1572864 | tf_op jit(solution)/shard_map/all_to_all | solution.py:398
  110.3 1.1 %restore.1 = bf16[128,3072]{1,0:T(8,128)(2,1)} custom-call(bf16[16,192,128]{2,1,0:T(8,128)(2,1)S(1)} %all_to_all.11.returned), custom_call_target="tpu_custom_call" | custom-call | tf_op jit(solution)/shard_map/restore/pallas_call | solution.py:401
Async XLA Ops:
  5.7 45.8 %copy-start = (s32[1,3]{1,0:T(1,128)S(1)}, s32[1,3]{1,0:T(1,128)}, u32[]{:S(2)}) copy-start(s32[1,3]{1,0:T(1,128)} %lengths.5) | copy-start | bytes 40
  49.5 9.7 %collective-permute-start = (bf16[16,704,128]{2,1,0:T(8,128)(2,1)S(1)}, bf16[16,704,128]{2,1,0:T(8,128)(2,1)S(1)}, u32[]{:S(2)}, u32[]{:S(2)}) collective-permute-start(bf16[16,704,128]{2,1,0:T(8,128)(2,1)S(1)} %all_to_all.10.own), channel_id=1, source_target_pairs={{0,1},{1,0},{2,3},{3,2},{4,5},{5,4},{6,7},{7,6},{8,9},{9,8},{10,11... | collective-permute-start | bytes 8650760 | tf_op jit(solution)/shard_map/ppermute | solution.py:360

commit v3 on v2

--- a/solution.py
+++ b/solution.py
@@ -45,7 +45,7 @@
 
 def prepare_kernel(
     lengths, latents, shift, scale, query, key, value, down, up, index, weight, send,
-    latents_in, query_in, key_in, value_in, down_in, up_in, stage, in_sems, out_sems,
+    latents_in, query_in, key_in, value_in, down_in, up_in, in_sems,
 ):
     pairs = (
         (latents, latents_in),
@@ -115,9 +115,6 @@
         load.wait()
     trio = 3 * HEAD_DIM
 
-    def post(chip):
-        return pltpu.make_async_copy(stage.at[chip], send.at[chip], out_sems.at[chip])
-
     for pair in range(CHIPS // 2):
         lanes = slice(pair * trio, (pair + 1) * trio)
         update = jnp.dot(scaled, up_in[:, lanes], preferred_element_type=jnp.float32)
@@ -127,15 +124,12 @@
             main, shared, row = heads_of(side)
             main_at, shared_at = columns(3 * pair + main), columns(3 * pair + shared)
             chip = 2 * pair + side
-            stage[chip, 0:ROWS] = query_in[:, main_at]
-            stage[chip, ROWS:Q_ROWS] = query_in[row : row + HALF, shared_at]
-            stage[chip, K_AT : K_AT + ROWS] = key_in[:, main_at]
-            stage[chip, K_AT + ROWS : V_AT] = key_in[:, shared_at]
-            stage[chip, V_AT : V_AT + ROWS] = turned[main]
-            stage[chip, V_AT + ROWS : PIECE] = turned[shared]
-            post(chip).start()
-    for chip in range(CHIPS):
-        post(chip).wait()
+            send[chip, 0:ROWS] = query_in[:, main_at]
+            send[chip, ROWS:Q_ROWS] = query_in[row : row + HALF, shared_at]
+            send[chip, K_AT : K_AT + ROWS] = key_in[:, main_at]
+            send[chip, K_AT + ROWS : V_AT] = key_in[:, shared_at]
+            send[chip, V_AT : V_AT + ROWS] = turned[main]
+            send[chip, V_AT + ROWS : PIECE] = turned[shared]
 
 
 def nt(left, right):
@@ -327,7 +321,7 @@
         prepare_kernel,
         out_shape=jax.ShapeDtypeStruct((CHIPS, PIECE, HEAD_DIM), wide),
         in_specs=[smem, anywhere, vmem, vmem] + [anywhere] * 5 + [vmem, vmem],
-        out_specs=anywhere,
+        out_specs=vmem,
         scratch_shapes=[
             pltpu.VMEM((ROWS, width), wide),
             pltpu.VMEM((ROWS, width), wide),
@@ -335,24 +329,27 @@
             pltpu.VMEM((ROWS, width), wide),
             pltpu.VMEM((width, ROWS), wide),
             pltpu.VMEM((ROWS, width), wide),
-            pltpu.VMEM((CHIPS, PIECE, HEAD_DIM), wide),
             dma((6,)),
-            dma((CHIPS,)),
         ],
-        compiler_params=pltpu.CompilerParams(vmem_limit_bytes=60 * 1024 * 1024),
+        compiler_params=params,
         name="prepare",
     )(
-        sequence_length,
-        latents[0],
-        modulation_shift[0],
-        modulation_scale[0],
-        query[0],
-        key[0],
-        value[0],
-        adapter_down_weight,
-        adapter_up_weight,
-        adapter_index[0].T,
-        adapter_weight[0].T,
+        *(
+            pltpu.with_memory_space_constraint(operand, pltpu.HBM)
+            for operand in (
+                sequence_length,
+                latents[0],
+                modulation_shift[0],
+                modulation_scale[0],
+                query[0],
+                key[0],
+                value[0],
+                adapter_down_weight,
+                adapter_up_weight,
+                adapter_index[0].T,
+                adapter_weight[0].T,
+            )
+        )
     )
     own = lax.all_to_all(
         send, "seq", split_axis=0, concat_axis=0, tiled=True, axis_index_groups=same_core

time: 112 us -> 110 us (0.982)
  Pallas kernels: 50.7 us -> 49.2 us
    pallas_call x1, Pallas kernels: 5.7 us -> 4.43 us  [body(): pl.pallas_call(prepare_kernel, out_shape=jax.ShapeDtypeStruct((CHIPS, PIE...]
where the time goes in v3:
time: 110 us
  blocking collectives  58.6 us (53%)
  Pallas kernels  49.2 us (45%)
  starting transfers between devices  1.91 us (2%)
    all_to_all x1, blocking collectives, body(): lax.all_to_all(send, 'seq', split_axis=0, concat_axis=0, tiled=True, axis...  43.6 us
    pallas_call x1, Pallas kernels, body(): pl.pallas_call(peer_kernel, out_shape=jax.ShapeDtypeStruct((CHIPS, Q_ROWS...  35.8 us
    all_to_all x1, blocking collectives, body(): lax.all_to_all(attended, 'seq', split_axis=0, concat_axis=0, tiled=True,...  15 us
    pallas_call x1, Pallas kernels, body(): pl.pallas_call(own_kernel, out_shape=[jax.ShapeDtypeStruct((TILES, HEAD_D...  7.85 us
    pallas_call x1, Pallas kernels, body(): pl.pallas_call(prepare_kernel, out_shape=jax.ShapeDtypeStruct((CHIPS, PIE...  4.43 us
  transfers between devices with their start and end apart: 1, of which 0 were waited for; matrix products, arithmetic and copies ran while one was open for 0% of the time, Pallas kernels for 7%

profile of v3, /device:TPU:480, one launch (start us, length us, event | category | flops | bytes accessed | tf_op | source)
XLA Modules:
  0.0 109.8 jit_solution(9830350478557668392)
XLA Ops:
  0.0 4.4 %prepare.1 = bf16[16,704,128]{2,1,0:T(8,128)(2,1)S(1)} custom-call(s32[1,3]{1,0:T(1,128)} %lengths.5, bf16[128,3072]{1,0:T(8,128)(2,1)} %bitcast.13, bf16[3,3072]{1,0:T(4,128)(2,1)} %bitcast.17, bf16[3,3072]{1,0:T(4,128)(2,1)} %bitcast.18, bf16[128,3072]{1,0:T(8,128)(2,1)} %bitcast.14, bf16[128,3072]{1,0:T(8,128)(2,1)} %bitcast.15, ...), custom_call_target="tpu_custom_call" | custom-call | tf_op jit(solution)/shard_map/prepare/pallas_call | solution.py:320
  4.4 0.0 copy-start
  4.4 43.6 %all_to_all.10.own = bf16[16,704,128]{2,1,0:T(8,128)(2,1)S(1)} all-to-all(bf16[16,704,128]{2,1,0:T(8,128)(2,1)S(1)} %prepare.1), channel_id=1, replica_groups={{0,2,4,6,8,10,12,14,16,18,20,22,24,26,28,30},{1,3,5,7,9,11,13,15,17,19,..., dimensions={0} | all-to-all | bytes 5767168 | tf_op jit(solution)/shard_map/all_to_all | solution.py:354
  48.1 1.9 %collective-permute-start = (bf16[16,704,128]{2,1,0:T(8,128)(2,1)S(1)}, bf16[16,704,128]{2,1,0:T(8,128)(2,1)S(1)}, u32[]{:S(2)}, u32[]{:S(2)}) collective-permute-start(bf16[16,704,128]{2,1,0:T(8,128)(2,1)S(1)} %all_to_all.10.own), channel_id=1, source_target_pairs={{0,1},{1,0},{2,3},{3,2},{4,5},{5,4},{6,7},{7,6},{8,9},{9,8},{10,11... | collective-permute-start | bytes 8650760 | tf_op jit(solution)/shard_map/ppermute | solution.py:357
  50.0 0.0 copy-done
  50.0 7.8 %attend_own.1 = (f32[6,128,512]{2,1,0:T(8,128)S(1)}, f32[6,8,512]{2,1,0:T(8,128)S(1)}, bf16[6,512,256]{2,1,0:T(8,128)(2,1)S(1)}, bf16[16,128,128]{2,1,0:T(8,128)(2,1)S(1)}) custom-call(s32[1,3]{1,0:T(1,128)S(1)} %copy-done, bf16[16,704,128]{2,1,0:T(8,128)(2,1)S(1)} %all_to_all.10.own), custom_call_target="tpu_custom_call" | custom-call | flops 4831838208 | bytes 4194304 | tf_op jit(solution)/shard_map/attend_own/pallas_call | solution.py:364
  57.8 0.0 collective-permute-done.peer
  57.9 35.8 %attend_peer.1 = bf16[16,192,128]{2,1,0:T(8,128)(2,1)S(1)} custom-call(s32[1,3]{1,0:T(1,128)S(1)} %copy-done, bf16[16,704,128]{2,1,0:T(8,128)(2,1)S(1)} %all_to_all.10.own, bf16[16,704,128]{2,1,0:T(8,128)(2,1)S(1)} %collective-permute-done.peer, f32[6,128,512]{2,1,0:T(8,128)S(1)} %get-tuple-element.9.accums, f32[6,8,512]{2,1,0:T(8,128)S(1)} %get-tuple-element.10.totals, ...), custom_call_target="tpu_custom_call" | custom-call | flops 4831838208 | bytes 4194304 | tf_op jit(solution)/shard_map/attend_peer/pallas_call | solution.py:379
  93.7 15.0 %all_to_all.11.returned = bf16[16,192,128]{2,1,0:T(8,128)(2,1)S(1)} all-to-all(bf16[16,192,128]{2,1,0:T(8,128)(2,1)S(1)} %attend_peer.1), channel_id=1, replica_groups={{0,2,4,6,8,10,12,14,16,18,20,22,24,26,28,30},{1,3,5,7,9,11,13,15,17,19,..., dimensions={0} | all-to-all | bytes 1572864 | tf_op jit(solution)/shard_map/all_to_all | solution.py:395
  108.7 1.1 %restore.1 = bf16[128,3072]{1,0:T(8,128)(2,1)} custom-call(bf16[16,192,128]{2,1,0:T(8,128)(2,1)S(1)} %all_to_all.11.returned), custom_call_target="tpu_custom_call" | custom-call | tf_op jit(solution)/shard_map/restore/pallas_call | solution.py:398
Async XLA Ops:
  4.4 45.5 %copy-start = (s32[1,3]{1,0:T(1,128)S(1)}, s32[1,3]{1,0:T(1,128)}, u32[]{:S(2)}) copy-start(s32[1,3]{1,0:T(1,128)} %lengths.5) | copy-start | bytes 40
  48.1 9.8 %collective-permute-start = (bf16[16,704,128]{2,1,0:T(8,128)(2,1)S(1)}, bf16[16,704,128]{2,1,0:T(8,128)(2,1)S(1)}, u32[]{:S(2)}, u32[]{:S(2)}) collective-permute-start(bf16[16,704,128]{2,1,0:T(8,128)(2,1)S(1)} %all_to_all.10.own), channel_id=1, source_target_pairs={{0,1},{1,0},{2,3},{3,2},{4,5},{5,4},{6,7},{7,6},{8,9},{9,8},{10,11... | collective-permute-start | bytes 8650760 | tf_op jit(solution)/shard_map/ppermute | solution.py:357

commit v4 on v3

--- a/solution.py
+++ b/solution.py
@@ -22,7 +22,7 @@
 V_AT = K_AT + 2 * ROWS
 PIECE = V_AT + 2 * ROWS
 KV_ROWS = 4 * ROWS
-TILE = 512
+TILE = 1024
 TILES = CHIPS * Q_ROWS // TILE
 STEP = 8
 SAFE_LOW, SAFE_HIGH = 2.0**-60, 2.0**100

time: 110 us -> 118 us (1.073)
  Pallas kernels: 49.2 us -> 56.9 us
    pallas_call x1, Pallas kernels: 35.8 us -> 44.2 us  [body(): pl.pallas_call(peer_kernel, out_shape=jax.ShapeDtypeStruct((CHIPS, Q_ROWS...]
  transfers between devices with their start and end apart: 1 -> 1, of which waited for: 0 -> 0; matrix products, arithmetic and copies ran while one was open for 0% -> 0% of each run, Pallas kernels for 7% -> 6%
where the time goes in v4:
time: 118 us; the launch traced here: 117 us
  blocking collectives  58.6 us (50%)
  Pallas kernels  56.9 us (48%)
  starting transfers between devices  1.91 us (2%)
    pallas_call x1, Pallas kernels, body(): pl.pallas_call(peer_kernel, out_shape=jax.ShapeDtypeStruct((CHIPS, Q_ROWS...  44.2 us
    all_to_all x1, blocking collectives, body(): lax.all_to_all(send, 'seq', split_axis=0, concat_axis=0, tiled=True, axis...  43.6 us
    all_to_all x1, blocking collectives, body(): lax.all_to_all(attended, 'seq', split_axis=0, concat_axis=0, tiled=True,...  15 us
    pallas_call x1, Pallas kernels, body(): pl.pallas_call(own_kernel, out_shape=[jax.ShapeDtypeStruct((TILES, HEAD_D...  7.14 us
    pallas_call x1, Pallas kernels, body(): pl.pallas_call(prepare_kernel, out_shape=jax.ShapeDtypeStruct((CHIPS, PIE...  4.43 us
  transfers between devices with their start and end apart: 1, of which 0 were waited for; matrix products, arithmetic and copies ran while one was open for 0% of the time, Pallas kernels for 6%

profile of v4, /device:TPU:480, one launch (start us, length us, event | category | flops | bytes accessed | tf_op | source)
XLA Modules:
  0.0 117.5 jit_solution(9571975989674372512)
XLA Ops:
  0.0 4.4 %prepare.1 = bf16[16,704,128]{2,1,0:T(8,128)(2,1)S(1)} custom-call(s32[1,3]{1,0:T(1,128)} %lengths.5, bf16[128,3072]{1,0:T(8,128)(2,1)} %bitcast.13, bf16[3,3072]{1,0:T(4,128)(2,1)} %bitcast.17, bf16[3,3072]{1,0:T(4,128)(2,1)} %bitcast.18, bf16[128,3072]{1,0:T(8,128)(2,1)} %bitcast.14, bf16[128,3072]{1,0:T(8,128)(2,1)} %bitcast.15, ...), custom_call_target="tpu_custom_call" | custom-call | tf_op jit(solution)/shard_map/prepare/pallas_call | solution.py:320
  4.4 0.0 copy-start
  4.4 43.6 %all_to_all.10.own = bf16[16,704,128]{2,1,0:T(8,128)(2,1)S(1)} all-to-all(bf16[16,704,128]{2,1,0:T(8,128)(2,1)S(1)} %prepare.1), channel_id=1, replica_groups={{0,2,4,6,8,10,12,14,16,18,20,22,24,26,28,30},{1,3,5,7,9,11,13,15,17,19,..., dimensions={0} | all-to-all | bytes 5767168 | tf_op jit(solution)/shard_map/all_to_all | solution.py:354
  48.1 1.9 %collective-permute-start = (bf16[16,704,128]{2,1,0:T(8,128)(2,1)S(1)}, bf16[16,704,128]{2,1,0:T(8,128)(2,1)S(1)}, u32[]{:S(2)}, u32[]{:S(2)}) collective-permute-start(bf16[16,704,128]{2,1,0:T(8,128)(2,1)S(1)} %all_to_all.10.own), channel_id=1, source_target_pairs={{0,1},{1,0},{2,3},{3,2},{4,5},{5,4},{6,7},{7,6},{8,9},{9,8},{10,11... | collective-permute-start | bytes 8650760 | tf_op jit(solution)/shard_map/ppermute | solution.py:357
  50.0 0.0 copy-done
  50.0 7.1 %attend_own.1 = (f32[3,128,1024]{2,1,0:T(8,128)S(1)}, f32[3,8,1024]{2,1,0:T(8,128)S(1)}, bf16[3,1024,256]{2,1,0:T(8,128)(2,1)S(1)}, bf16[16,128,128]{2,1,0:T(8,128)(2,1)S(1)}) custom-call(s32[1,3]{1,0:T(1,128)S(1)} %copy-done, bf16[16,704,128]{2,1,0:T(8,128)(2,1)S(1)} %all_to_all.10.own), custom_call_target="tpu_custom_call" | custom-call | flops 4831838208 | bytes 4194304 | tf_op jit(solution)/shard_map/attend_own/pallas_call | solution.py:364
  57.1 0.0 collective-permute-done.peer
  57.1 44.2 %attend_peer.1 = bf16[16,192,128]{2,1,0:T(8,128)(2,1)S(1)} custom-call(s32[1,3]{1,0:T(1,128)S(1)} %copy-done, bf16[16,704,128]{2,1,0:T(8,128)(2,1)S(1)} %all_to_all.10.own, bf16[16,704,128]{2,1,0:T(8,128)(2,1)S(1)} %collective-permute-done.peer, f32[3,128,1024]{2,1,0:T(8,128)S(1)} %get-tuple-element.9.accums, f32[3,8,1024]{2,1,0:T(8,128)S(1)} %get-tuple-element.10.totals, ...), custom_call_target="tpu_custom_call" | custom-call | flops 4831838208 | bytes 4194304 | tf_op jit(solution)/shard_map/attend_peer/pallas_call | solution.py:379
  101.4 15.0 %all_to_all.11.returned = bf16[16,192,128]{2,1,0:T(8,128)(2,1)S(1)} all-to-all(bf16[16,192,128]{2,1,0:T(8,128)(2,1)S(1)} %attend_peer.1), channel_id=1, replica_groups={{0,2,4,6,8,10,12,14,16,18,20,22,24,26,28,30},{1,3,5,7,9,11,13,15,17,19,..., dimensions={0} | all-to-all | bytes 1572864 | tf_op jit(solution)/shard_map/all_to_all | solution.py:395
  116.3 1.1 restore.1
Async XLA Ops:
  4.4 45.5 %copy-start = (s32[1,3]{1,0:T(1,128)S(1)}, s32[1,3]{1,0:T(1,128)}, u32[]{:S(2)}) copy-start(s32[1,3]{1,0:T(1,128)} %lengths.5) | copy-start | bytes 40
  48.1 9.1 %collective-permute-start = (bf16[16,704,128]{2,1,0:T(8,128)(2,1)S(1)}, bf16[16,704,128]{2,1,0:T(8,128)(2,1)S(1)}, u32[]{:S(2)}, u32[]{:S(2)}) collective-permute-start(bf16[16,704,128]{2,1,0:T(8,128)(2,1)S(1)} %all_to_all.10.own), channel_id=1, source_target_pairs={{0,1},{1,0},{2,3},{3,2},{4,5},{5,4},{6,7},{7,6},{8,9},{9,8},{10,11... | collective-permute-start | bytes 8650760 | tf_op jit(solution)/shard_map/ppermute | solution.py:357

commit v5 on v4

--- a/solution.py
+++ b/solution.py
@@ -24,7 +24,7 @@
 KV_ROWS = 4 * ROWS
 TILE = 1024
 TILES = CHIPS * Q_ROWS // TILE
-STEP = 8
+STEP = 16
 SAFE_LOW, SAFE_HIGH = 2.0**-60, 2.0**100
 
 mask_value = -1e30

time: 118 us -> 118 us (level)
  no operation moved by 1% of the time
where the time goes in v5:
time: 118 us; the launch traced here: 117 us
  blocking collectives  58.6 us (50%)
  Pallas kernels  56.9 us (48%)
  starting transfers between devices  1.91 us (2%)
    pallas_call x1, Pallas kernels, body(): pl.pallas_call(peer_kernel, out_shape=jax.ShapeDtypeStruct((CHIPS, Q_ROWS...  44.2 us
    all_to_all x1, blocking collectives, body(): lax.all_to_all(send, 'seq', split_axis=0, concat_axis=0, tiled=True, axis...  43.6 us
    all_to_all x1, blocking collectives, body(): lax.all_to_all(attended, 'seq', split_axis=0, concat_axis=0, tiled=True,...  15 us
    pallas_call x1, Pallas kernels, body(): pl.pallas_call(own_kernel, out_shape=[jax.ShapeDtypeStruct((TILES, HEAD_D...  7.17 us
    pallas_call x1, Pallas kernels, body(): pl.pallas_call(prepare_kernel, out_shape=jax.ShapeDtypeStruct((CHIPS, PIE...  4.43 us
  transfers between devices with their start and end apart: 1, of which 0 were waited for; matrix products, arithmetic and copies ran while one was open for 0% of the time, Pallas kernels for 6%

profile of v5, /device:TPU:480, one launch (start us, length us, event | category | flops | bytes accessed | tf_op | source)
XLA Modules:
  0.0 117.5 jit_solution(3219457914925858042)
XLA Ops:
  0.0 4.4 %prepare.1 = bf16[16,704,128]{2,1,0:T(8,128)(2,1)S(1)} custom-call(s32[1,3]{1,0:T(1,128)} %lengths.5, bf16[128,3072]{1,0:T(8,128)(2,1)} %bitcast.13, bf16[3,3072]{1,0:T(4,128)(2,1)} %bitcast.17, bf16[3,3072]{1,0:T(4,128)(2,1)} %bitcast.18, bf16[128,3072]{1,0:T(8,128)(2,1)} %bitcast.14, bf16[128,3072]{1,0:T(8,128)(2,1)} %bitcast.15, ...), custom_call_target="tpu_custom_call" | custom-call | tf_op jit(solution)/shard_map/prepare/pallas_call | solution.py:320
  4.4 0.0 copy-start
  4.4 43.6 %all_to_all.10.own = bf16[16,704,128]{2,1,0:T(8,128)(2,1)S(1)} all-to-all(bf16[16,704,128]{2,1,0:T(8,128)(2,1)S(1)} %prepare.1), channel_id=1, replica_groups={{0,2,4,6,8,10,12,14,16,18,20,22,24,26,28,30},{1,3,5,7,9,11,13,15,17,19,..., dimensions={0} | all-to-all | bytes 5767168 | tf_op jit(solution)/shard_map/all_to_all | solution.py:354
  48.1 1.9 %collective-permute-start = (bf16[16,704,128]{2,1,0:T(8,128)(2,1)S(1)}, bf16[16,704,128]{2,1,0:T(8,128)(2,1)S(1)}, u32[]{:S(2)}, u32[]{:S(2)}) collective-permute-start(bf16[16,704,128]{2,1,0:T(8,128)(2,1)S(1)} %all_to_all.10.own), channel_id=1, source_target_pairs={{0,1},{1,0},{2,3},{3,2},{4,5},{5,4},{6,7},{7,6},{8,9},{9,8},{10,11... | collective-permute-start | bytes 8650760 | tf_op jit(solution)/shard_map/ppermute | solution.py:357
  50.0 0.0 copy-done
  50.0 7.2 %attend_own.1 = (f32[3,128,1024]{2,1,0:T(8,128)S(1)}, f32[3,8,1024]{2,1,0:T(8,128)S(1)}, bf16[3,1024,256]{2,1,0:T(8,128)(2,1)S(1)}, bf16[16,128,128]{2,1,0:T(8,128)(2,1)S(1)}) custom-call(s32[1,3]{1,0:T(1,128)S(1)} %copy-done, bf16[16,704,128]{2,1,0:T(8,128)(2,1)S(1)} %all_to_all.10.own), custom_call_target="tpu_custom_call" | custom-call | flops 4831838208 | bytes 4194304 | tf_op jit(solution)/shard_map/attend_own/pallas_call | solution.py:364
  57.2 0.0 collective-permute-done.peer
  57.2 44.2 %attend_peer.1 = bf16[16,192,128]{2,1,0:T(8,128)(2,1)S(1)} custom-call(s32[1,3]{1,0:T(1,128)S(1)} %copy-done, bf16[16,704,128]{2,1,0:T(8,128)(2,1)S(1)} %all_to_all.10.own, bf16[16,704,128]{2,1,0:T(8,128)(2,1)S(1)} %collective-permute-done.peer, f32[3,128,1024]{2,1,0:T(8,128)S(1)} %get-tuple-element.9.accums, f32[3,8,1024]{2,1,0:T(8,128)S(1)} %get-tuple-element.10.totals, ...), custom_call_target="tpu_custom_call" | custom-call | flops 4831838208 | bytes 4194304 | tf_op jit(solution)/shard_map/attend_peer/pallas_call | solution.py:379
  101.3 15.0 %all_to_all.11.returned = bf16[16,192,128]{2,1,0:T(8,128)(2,1)S(1)} all-to-all(bf16[16,192,128]{2,1,0:T(8,128)(2,1)S(1)} %attend_peer.1), channel_id=1, replica_groups={{0,2,4,6,8,10,12,14,16,18,20,22,24,26,28,30},{1,3,5,7,9,11,13,15,17,19,..., dimensions={0} | all-to-all | bytes 1572864 | tf_op jit(solution)/shard_map/all_to_all | solution.py:395
  116.3 1.1 restore.1
Async XLA Ops:
  4.4 45.5 %copy-start = (s32[1,3]{1,0:T(1,128)S(1)}, s32[1,3]{1,0:T(1,128)}, u32[]{:S(2)}) copy-start(s32[1,3]{1,0:T(1,128)} %lengths.5) | copy-start | bytes 40
  48.1 9.1 %collective-permute-start = (bf16[16,704,128]{2,1,0:T(8,128)(2,1)S(1)}, bf16[16,704,128]{2,1,0:T(8,128)(2,1)S(1)}, u32[]{:S(2)}, u32[]{:S(2)}) collective-permute-start(bf16[16,704,128]{2,1,0:T(8,128)(2,1)S(1)} %all_to_all.10.own), channel_id=1, source_target_pairs={{0,1},{1,0},{2,3},{3,2},{4,5},{5,4},{6,7},{7,6},{8,9},{9,8},{10,11... | collective-permute-start | bytes 8650760 | tf_op jit(solution)/shard_map/ppermute | solution.py:357
